TPU v7x, 32 devices: a whole 2x2x4 slice. The times are simulated.
32 devices in a mesh: clip: 4 (over x, core), ctx: 2 (over y), tp: 4 (over z).
Axes of the slice: x: 2, y: 2, z: 4, core: 2. Of those that a mesh axis runs over, the one named last changes fastest.
Arguments:
- frames: bfloat16 [4096, 768], P(('clip', 'ctx')), may hold values from -6 to 6
- cotangent: bfloat16 [4096, 768], P(('clip', 'ctx')), may hold values from -6 to 6
- first_gain: bfloat16 [768], P('clip'), may hold values from 0.099609375 to 1.8984375
- first_shift: bfloat16 [768], P('clip'), may hold values from -3 to 3
- query_weight: bfloat16 [768, 768], P('clip', 'tp'), may hold values from -0.21875 to 0.21875
- query_bias: bfloat16 [768], P('tp'), may hold values from -3 to 3
- key_weight: bfloat16 [768, 768], P('clip', 'tp'), may hold values from -0.21875 to 0.21875
- value_weight: bfloat16 [768, 768], P('clip', 'tp'), may hold values from -0.21875 to 0.21875
- value_bias: bfloat16 [768], P('tp'), may hold values from -3 to 3
- out_weight: bfloat16 [768, 768], P('tp', 'clip'), may hold values from -1.75 to 1.75
- out_bias: bfloat16 [768], P('clip'), may hold values from -3 to 3
- second_gain: bfloat16 [768], P('clip'), may hold values from 0.099609375 to 1.8984375
- second_shift: bfloat16 [768], P('clip'), may hold values from -3 to 3
- expand_weight: bfloat16 [768, 3072], P('clip', 'tp'), may hold values from -0.21875 to 0.21875
- expand_bias: bfloat16 [3072], P('tp'), may hold values from -3 to 3
- reduce_weight: bfloat16 [3072, 768], P('tp', 'clip'), may hold values from -0.109375 to 0.109375
- reduce_bias: bfloat16 [768], P('clip'), may hold values from -3 to 3
Outputs:
- layer_out: bfloat16 [4096, 768], P(('clip', 'ctx'))
- frames_grad: float32 [4096, 768], P(('clip', 'ctx'))
- first_gain_grad: float32 [768], P('clip')
- first_shift_grad: float32 [768], P('clip')
- query_weight_grad: float32 [768, 768], P('clip', 'tp')
- query_bias_grad: float32 [768], P('tp')
- key_weight_grad: float32 [768, 768], P('clip', 'tp')
- value_weight_grad: float32 [768, 768], P('clip', 'tp')
- value_bias_grad: float32 [768], P('tp')
- out_weight_grad: float32 [768, 768], P('tp', 'clip')
- out_bias_grad: float32 [768], P('clip')
- second_gain_grad: float32 [768], P('clip')
- second_shift_grad: float32 [768], P('clip')
- expand_weight_grad: float32 [768, 3072], P('clip', 'tp')
- expand_bias_grad: float32 [3072], P('tp')
- reduce_weight_grad: float32 [3072, 768], P('tp', 'clip')
- reduce_bias_grad: float32 [768], P('clip')
All inputs are finite; a program needn't handle non-finite values.
Results may differ from a plain program's by a relative error of at most 0.023.
Values may be sent and summed in bfloat16 or wider, within the bound.
A program may use at most 128 MiB of HBM per device.

v0:
```python
import jax
import jax.numpy as jnp
from jax import lax
from jax.sharding import PartitionSpec as P

DH = 64


def center_rows(matrix):
    row_mean = jnp.mean(matrix, axis=-1, keepdims=True)
    centred = matrix - row_mean
    factor = lax.rsqrt(jnp.mean(centred * centred, axis=-1, keepdims=True) + 1e-05)
    return (centred * factor, factor)


def norm_back(grad_norm, normed, factor, gain):
    grad_hat = grad_norm * gain
    inner = jnp.mean(grad_hat, axis=-1, keepdims=True)
    cross = jnp.mean(grad_hat * normed, axis=-1, keepdims=True)
    return factor * (grad_hat - inner - normed * cross)


def product(left, right):
    return jnp.dot(left, right, preferred_element_type=jnp.float32)


def rows_inner(left, right):
    return lax.dot_general(
        left, right, (((0,), (0,)), ((), ())), preferred_element_type=jnp.float32
    )


def cols_inner(left, right):
    return lax.dot_general(
        left, right, (((1,), (1,)), ((), ())), preferred_element_type=jnp.float32
    )


def score_block(query_heads, key_heads, value_heads, grad_heads, log_total, row_delta, score_scale):
    scores = (
        jnp.einsum("qhd,khd->qhk", query_heads, key_heads, preferred_element_type=jnp.float32)
        * score_scale
    )
    weights = jnp.exp(scores - log_total[..., None])
    grad_weights = jnp.einsum(
        "qhd,khd->qhk", grad_heads, value_heads, preferred_element_type=jnp.float32
    )
    grad_scores = (weights * (grad_weights - row_delta[..., None])).astype(jnp.bfloat16)
    return (weights.astype(jnp.bfloat16), grad_scores)


def shards(
    frames,
    cotangent,
    first_gain,
    first_shift,
    query_weight,
    query_bias,
    key_weight,
    value_weight,
    value_bias,
    out_weight,
    out_bias,
    second_gain,
    second_shift,
    expand_weight,
    expand_bias,
    reduce_weight,
    reduce_bias,
):
    row_count = frames.shape[0]
    local_width = query_weight.shape[1]
    head_count = local_width // DH
    score_scale = DH ** (-0.5)
    query_full, key_full, value_full, out_full, out_shift, gain_first, shift_first = (
        lax.all_gather(query_weight, "clip", axis=0, tiled=True),
        lax.all_gather(key_weight, "clip", axis=0, tiled=True),
        lax.all_gather(value_weight, "clip", axis=0, tiled=True),
        lax.all_gather(out_weight, "clip", axis=1, tiled=True),
        lax.all_gather(out_bias, "clip", axis=0, tiled=True),
        lax.all_gather(first_gain, "clip", axis=0, tiled=True),
        lax.all_gather(first_shift, "clip", axis=0, tiled=True),
    )
    inputs = frames.astype(jnp.float32)
    normed_one, factor_one = center_rows(inputs)
    first_norm = (
        normed_one * gain_first.astype(jnp.float32) + shift_first.astype(jnp.float32)
    ).astype(jnp.bfloat16)
    queries = (product(first_norm, query_full) + query_bias.astype(jnp.float32)).astype(
        jnp.bfloat16
    )
    key_rows = product(first_norm, key_full).astype(jnp.bfloat16)
    value_rows = (product(first_norm, value_full) + value_bias.astype(jnp.float32)).astype(
        jnp.bfloat16
    )
    query_heads = queries.reshape(row_count, head_count, DH)
    start_max = jnp.full((row_count, head_count), -1e30, jnp.float32)
    pieces = (
        lax.all_gather(key_rows, "ctx", axis=0, tiled=True),
        lax.all_gather(value_rows, "ctx", axis=0, tiled=True),
    )
    run_max = start_max
    length = pieces[0].shape[0]
    key_heads = pieces[0].reshape(length, head_count, DH)
    value_heads = pieces[1].reshape(length, head_count, DH)
    scores = (
        jnp.einsum("qhd,khd->qhk", query_heads, key_heads, preferred_element_type=jnp.float32)
        * score_scale
    )
    new_max = jnp.maximum(run_max, jnp.max(scores, axis=-1))
    weights = jnp.exp(scores - new_max[..., None])
    run_sum = jnp.sum(weights, axis=-1)
    run_acc = jnp.einsum(
        "qhk,khd->qhd",
        weights.astype(jnp.bfloat16),
        value_heads,
        preferred_element_type=jnp.float32,
    )
    run_max, run_sum, run_acc = (new_max, run_sum, run_acc)
    mixed_full = run_acc / run_sum[..., None]
    log_total = run_max + jnp.log(run_sum)
    mixed_low = mixed_full.reshape(row_count, local_width).astype(jnp.bfloat16)
    attn_sum = lax.psum(product(mixed_low, out_full).astype(jnp.bfloat16), "tp").astype(jnp.float32)
    hidden = inputs + attn_sum + out_shift.astype(jnp.float32)
    expand_full, reduce_full, reduce_shift, gain_second, shift_second = (
        lax.all_gather(expand_weight, "clip", axis=0, tiled=True),
        lax.all_gather(reduce_weight, "clip", axis=1, tiled=True),
        lax.all_gather(reduce_bias, "clip", axis=0, tiled=True),
        lax.all_gather(second_gain, "clip", axis=0, tiled=True),
        lax.all_gather(second_shift, "clip", axis=0, tiled=True),
    )
    normed_two, factor_two = center_rows(hidden)
    second_norm = (
        normed_two * gain_second.astype(jnp.float32) + shift_second.astype(jnp.float32)
    ).astype(jnp.bfloat16)
    pre_act = product(second_norm, expand_full) + expand_bias.astype(jnp.float32)

    def gelu_exact(argument):
        return jax.nn.gelu(argument, approximate=False)

    activated, gelu_pull = jax.vjp(gelu_exact, pre_act)
    act_low = activated.astype(jnp.bfloat16)
    mlp_sum = lax.psum(product(act_low, reduce_full).astype(jnp.bfloat16), "tp").astype(jnp.float32)
    layer_out = (hidden + mlp_sum + reduce_shift.astype(jnp.float32)).astype(jnp.bfloat16)
    grad_out = cotangent.astype(jnp.float32)
    grad_reduce = rows_inner(act_low, cotangent)
    grad_reduce_bias = jnp.sum(grad_out, axis=0)
    grad_act = cols_inner(cotangent, reduce_full)
    grad_pre = gelu_pull(grad_act)[0].astype(jnp.bfloat16)
    grad_expand = rows_inner(second_norm, grad_pre)
    grad_expand_bias = jnp.sum(grad_pre.astype(jnp.float32), axis=0)
    grad_second = lax.psum(cols_inner(grad_pre, expand_full).astype(jnp.bfloat16), "tp").astype(
        jnp.float32
    )
    grad_gain_two = jnp.sum(grad_second * normed_two, axis=0)
    grad_shift_two = jnp.sum(grad_second, axis=0)
    grad_hidden = grad_out + norm_back(
        grad_second, normed_two, factor_two, gain_second.astype(jnp.float32)
    )
    grad_attn = grad_hidden.astype(jnp.bfloat16)
    grad_out_weight = rows_inner(mixed_low, grad_attn)
    grad_out_bias = jnp.sum(grad_attn.astype(jnp.float32), axis=0)
    grad_mixed = cols_inner(grad_attn, out_full).astype(jnp.bfloat16)
    grad_heads = grad_mixed.reshape(row_count, head_count, DH)
    row_delta = jnp.sum(grad_heads.astype(jnp.float32) * mixed_full, axis=-1)
    pieces = (
        lax.all_gather(key_rows, "ctx", axis=0, tiled=True),
        lax.all_gather(value_rows, "ctx", axis=0, tiled=True),
    )
    length = pieces[0].shape[0]
    key_heads = pieces[0].reshape(length, head_count, DH)
    value_heads = pieces[1].reshape(length, head_count, DH)
    weights_low, grad_scores = score_block(
        query_heads, key_heads, value_heads, grad_heads, log_total, row_delta, score_scale
    )
    grad_query = jnp.einsum(
        "qhk,khd->qhd", grad_scores, key_heads, preferred_element_type=jnp.float32
    )
    key_term = jnp.einsum(
        "qhk,qhd->khd", grad_scores, query_heads, preferred_element_type=jnp.float32
    )
    value_term = jnp.einsum(
        "qhk,qhd->khd", weights_low, grad_heads, preferred_element_type=jnp.float32
    )
    grad_key = key_term
    grad_value = value_term
    folded = (grad_query, grad_key, grad_value)
    grad_query = folded[0]
    grad_key, grad_value = (
        lax.psum_scatter(
            folded[1].astype(jnp.bfloat16), "ctx", scatter_dimension=0, tiled=True
        ).astype(jnp.float32),
        lax.psum_scatter(
            folded[2].astype(jnp.bfloat16), "ctx", scatter_dimension=0, tiled=True
        ).astype(jnp.float32),
    )
    grad_q_low = (grad_query * score_scale).reshape(row_count, local_width).astype(jnp.bfloat16)
    grad_k_low = (grad_key * score_scale).reshape(row_count, local_width).astype(jnp.bfloat16)
    grad_v_low = grad_value.reshape(row_count, local_width).astype(jnp.bfloat16)
    grad_query_weight = rows_inner(first_norm, grad_q_low)
    grad_key_weight = rows_inner(first_norm, grad_k_low)
    grad_value_weight = rows_inner(first_norm, grad_v_low)
    grad_query_bias = jnp.sum(grad_q_low.astype(jnp.float32), axis=0)
    grad_value_bias = jnp.sum(grad_v_low.astype(jnp.float32), axis=0)
    first_terms = (
        cols_inner(grad_q_low, query_full)
        + cols_inner(grad_k_low, key_full)
        + cols_inner(grad_v_low, value_full)
    )
    grad_first = lax.psum(first_terms.astype(jnp.bfloat16), "tp").astype(jnp.float32)
    grad_gain_one = jnp.sum(grad_first * normed_one, axis=0)
    grad_shift_one = jnp.sum(grad_first, axis=0)
    frames_grad = grad_hidden + norm_back(
        grad_first, normed_one, factor_one, gain_first.astype(jnp.float32)
    )
    shares = (
        lax.psum_scatter(
            grad_query_weight.astype(jnp.bfloat16), "clip", scatter_dimension=0, tiled=True
        ).astype(jnp.float32),
        lax.psum_scatter(
            grad_key_weight.astype(jnp.bfloat16), "clip", scatter_dimension=0, tiled=True
        ).astype(jnp.float32),
        lax.psum_scatter(
            grad_value_weight.astype(jnp.bfloat16), "clip", scatter_dimension=0, tiled=True
        ).astype(jnp.float32),
        lax.psum_scatter(
            grad_out_weight.astype(jnp.bfloat16), "clip", scatter_dimension=1, tiled=True
        ).astype(jnp.float32),
        lax.psum_scatter(
            grad_out_bias.astype(jnp.bfloat16), "clip", scatter_dimension=0, tiled=True
        ).astype(jnp.float32),
        lax.psum_scatter(
            grad_gain_one.astype(jnp.bfloat16), "clip", scatter_dimension=0, tiled=True
        ).astype(jnp.float32),
        lax.psum_scatter(
            grad_shift_one.astype(jnp.bfloat16), "clip", scatter_dimension=0, tiled=True
        ).astype(jnp.float32),
        lax.psum_scatter(
            grad_expand.astype(jnp.bfloat16), "clip", scatter_dimension=0, tiled=True
        ).astype(jnp.float32),
        lax.psum_scatter(
            grad_reduce.astype(jnp.bfloat16), "clip", scatter_dimension=1, tiled=True
        ).astype(jnp.float32),
        lax.psum_scatter(
            grad_reduce_bias.astype(jnp.bfloat16), "clip", scatter_dimension=0, tiled=True
        ).astype(jnp.float32),
        lax.psum_scatter(
            grad_gain_two.astype(jnp.bfloat16), "clip", scatter_dimension=0, tiled=True
        ).astype(jnp.float32),
        lax.psum_scatter(
            grad_shift_two.astype(jnp.bfloat16), "clip", scatter_dimension=0, tiled=True
        ).astype(jnp.float32),
    )
    (
        share_query,
        share_key,
        share_value,
        share_out,
        share_out_bias,
        share_gain_one,
        share_shift_one,
        share_expand,
        share_reduce,
        share_reduce_bias,
        share_gain_two,
        share_shift_two,
    ) = shares
    summed = (
        lax.psum(share_query.astype(jnp.bfloat16), "ctx").astype(jnp.float32),
        lax.psum(share_key.astype(jnp.bfloat16), "ctx").astype(jnp.float32),
        lax.psum(share_value.astype(jnp.bfloat16), "ctx").astype(jnp.float32),
        lax.psum(share_out.astype(jnp.bfloat16), "ctx").astype(jnp.float32),
        lax.psum(share_out_bias.astype(jnp.bfloat16), "ctx").astype(jnp.float32),
        lax.psum(share_gain_one.astype(jnp.bfloat16), "ctx").astype(jnp.float32),
        lax.psum(share_shift_one.astype(jnp.bfloat16), "ctx").astype(jnp.float32),
        lax.psum(share_expand.astype(jnp.bfloat16), "ctx").astype(jnp.float32),
        lax.psum(share_reduce.astype(jnp.bfloat16), "ctx").astype(jnp.float32),
        lax.psum(share_reduce_bias.astype(jnp.bfloat16), "ctx").astype(jnp.float32),
        lax.psum(share_gain_two.astype(jnp.bfloat16), "ctx").astype(jnp.float32),
        lax.psum(share_shift_two.astype(jnp.bfloat16), "ctx").astype(jnp.float32),
    )
    (
        sum_query,
        sum_key,
        sum_value,
        sum_out,
        sum_out_bias,
        sum_gain_one,
        sum_shift_one,
        sum_expand,
        sum_reduce,
        sum_reduce_bias,
        sum_gain_two,
        sum_shift_two,
    ) = summed
    bias_query, bias_value, bias_expand = lax.psum(
        (grad_query_bias, grad_value_bias, grad_expand_bias), ("clip", "ctx")
    )
    return (
        layer_out,
        frames_grad,
        sum_gain_one,
        sum_shift_one,
        sum_query,
        bias_query,
        sum_key,
        sum_value,
        bias_value,
        sum_out,
        sum_out_bias,
        sum_gain_two,
        sum_shift_two,
        sum_expand,
        bias_expand,
        sum_reduce,
        sum_reduce_bias,
    )


def solution(mesh):
    placed = (
        P(("clip", "ctx"), None),
        P(("clip", "ctx"), None),
        P("clip"),
        P("clip"),
        P("clip", "tp"),
        P("tp"),
        P("clip", "tp"),
        P("clip", "tp"),
        P("tp"),
        P("tp", "clip"),
        P("clip"),
        P("clip"),
        P("clip"),
        P("clip", "tp"),
        P("tp"),
        P("tp", "clip"),
        P("clip"),
    )
    return jax.shard_map(
        shards,
        mesh=mesh,
        in_specs=placed,
        out_specs=(
            P(("clip", "ctx"), None),
            P(("clip", "ctx"), None),
            P("clip"),
            P("clip"),
            P("clip", "tp"),
            P("tp"),
            P("clip", "tp"),
            P("clip", "tp"),
            P("tp"),
            P("tp", "clip"),
            P("clip"),
            P("clip"),
            P("clip"),
            P("clip", "tp"),
            P("tp"),
            P("tp", "clip"),
            P("clip"),
        ),
        check_vma=False,
    )
```

profile of v0, /device:TPU:0, one launch (start us, length us, event | category | flops | bytes accessed | tf_op | source)
XLA Modules:
  0.0 504.9 jit_solution(17064030569401417652)
XLA Ops:
  8.2 0.7 convert_element_type.253
  9.6 1.3 convert_reduce_fusion
  11.0 1.6 fusion.28
  15.0 12.6 %all-reduce.15 = (bf16[768]{0:T(1024)(128)(2,1)S(1)}, bf16[768]{0:T(1024)(128)(2,1)S(1)}, bf16[768]{0:T(1024)(128)(2,1)S(1)}, bf16[768]{0:T(1024)(128)(2,1)S(1)}, bf16[768]{0:T(1024)(128)(2,1)S(1)}) all-reduce(bf16[768]{0:T(1024)(128)(2,1)S(1)} %dynamic-update-slice.4, ...), channel_id=1, replica_groups=mesh['clip'=4,'ctx'=2,'tp'=4] {'clip'}, use_global_device_ids=true, to_apply=%add.4 | all-reduce | flops 3840 | bytes 15360
  27.7 6.1 %all_gather.51 = bf16[192,768]{0,1:T(8,128)(2,1)S(1)} all-gather(bf16[192,192]{0,1:T(8,128)(2,1)S(1)} %copy.39), channel_id=1, replica_groups=mesh['clip'=4,'ctx'=2,'tp'=4] {'clip'}, dimensions={1}, use_global_device_ids=true | all-gather | bytes 368640 | tf_op jit(solution)/shard_map/all_gather | solution.py:79
  33.9 6.6 %all_gather.50 = bf16[768,192]{1,0:T(8,128)(2,1)S(1)} all-gather(bf16[192,192]{1,0:T(8,128)(2,1)S(1)} %copy-done.29), channel_id=1, replica_groups=mesh['clip'=4,'ctx'=2,'tp'=4] {'clip'}, dimensions={0}, use_global_device_ids=true | all-gather | bytes 368640 | tf_op jit(solution)/shard_map/all_gather | solution.py:76
  40.5 6.6 %all_gather.48 = bf16[768,192]{1,0:T(8,128)(2,1)S(1)} all-gather(bf16[192,192]{1,0:T(8,128)(2,1)S(1)} %copy-done.30), channel_id=1, replica_groups=mesh['clip'=4,'ctx'=2,'tp'=4] {'clip'}, dimensions={0}, use_global_device_ids=true | all-gather | bytes 368640 | tf_op jit(solution)/shard_map/all_gather | solution.py:77
  47.0 6.6 %all_gather.46 = bf16[768,192]{1,0:T(8,128)(2,1)S(1)} all-gather(bf16[192,192]{1,0:T(8,128)(2,1)S(1)} %copy-done.31), channel_id=1, replica_groups=mesh['clip'=4,'ctx'=2,'tp'=4] {'clip'}, dimensions={0}, use_global_device_ids=true | all-gather | bytes 368640 | tf_op jit(solution)/shard_map/all_gather | solution.py:78
  54.4 7.8 %all_gather.47 = bf16[1024,192]{0,1:T(8,128)(2,1)S(1)} all-gather(bf16[512,192]{0,1:T(8,128)(2,1)S(1)} %fusion.54), channel_id=1, replica_groups=mesh['clip'=4,'ctx'=2,'tp'=4] {'ctx'}, dimensions={0}, use_global_device_ids=true | all-gather | bytes 589824 | tf_op jit(solution)/shard_map/all_gather | solution.py:100
  62.6 7.0 %all_gather.49 = bf16[1024,192]{0,1:T(8,128)(2,1)S(1)} all-gather(bf16[512,192]{0,1:T(8,128)(2,1)S(1)} %convolution_convert_fusion.11), channel_id=1, replica_groups=mesh['clip'=4,'ctx'=2,'tp'=4] {'ctx'}, dimensions={0}, use_global_device_ids=true | all-gather | bytes 589824 | tf_op jit(solution)/shard_map/all_gather | solution.py:99
  70.1 1.0 bitcast_reduce_fusion
  71.8 1.0 fusion.5
  72.8 1.0 copy-done
  73.8 1.9 fusion.67
  76.4 1.3 convolution_convert_fusion.4
  80.9 41.2 %all-reduce.23.cloned.1.call-done = bf16[512,768]{1,0:T(8,128)(2,1)} async-done(((bf16[512,768]{1,0:T(8,128)(2,1)}), bf16[512,768]{1,0:T(8,128)(2,1)}) %all-reduce.23.cloned.1.call-update) | async-done | bytes 786448 | tf_op jit(solution)/shard_map/psum | solution.py:123
  122.2 1.5 fusion.59
  124.8 3.5 convolution_add_fusion
  128.4 7.3 %convert_reduce_fusion.1 = (f32[768]{0:T(1024)}, bf16[512,768]{1,0:T(8,128)(2,1)S(1)}, f32[512,768]{1,0:T(8,128)}) fusion(f32[512,768]{1,0:T(8,128)} %convolution_add_fusion, bf16[512,768]{1,0:T(8,128)(2,1)S(1)} %copy-done.24, bf16[768,768]{0,1:T(8,128)(2,1)} %all-gather.5.cloned.1.call-done), kind=kOutput, calls=%fused_computation.48 | convolution fusion | flops 633076992 | bytes 5901312 | tf_op jit(solution)/shard_map/dot_general | solution.py:34
  135.7 0.9 copy-done.62
  136.6 1.7 convolution_convert_fusion.2
  138.9 42.5 %all-reduce.25.cloned.1.call-done = bf16[512,768]{1,0:T(8,128)(2,1)} async-done(((bf16[512,768]{1,0:T(8,128)(2,1)}), bf16[512,768]{1,0:T(8,128)(2,1)}) %all-reduce.25.cloned.1.call-update) | async-done | bytes 786448 | tf_op jit(solution)/shard_map/psum | solution.py:152
  181.5 2.7 fusion.33
  184.2 3.3 convert_reduce_fusion.4
  189.2 4.8 fusion.47
  194.0 4.6 fusion.1
  198.7 1.6 copy-done.2
  200.3 1.8 fusion.46
  202.2 2.0 convolution_convert_fusion.9
  204.2 1.9 copy.47
  206.2 3.2 convert_reduce_fusion.3
  209.4 0.7 copy-done.17
  210.1 1.2 convolution_convert_fusion.7
  211.3 2.1 convolution_convert_fusion.5
  213.8 8.8 %reduce-scatter.11.cloned.1.call-done = bf16[512,3,64]{0,2,1:T(8,128)(2,1)} async-done(((bf16[1024,3,64]{0,2,1:T(8,128)(2,1)}), bf16[512,3,64]{0,2,1:T(8,128)(2,1)}) %reduce-scatter.11.cloned.1.call-update) | async-done | bytes 196624 | tf_op jit(solution)/shard_map/reduce_scatter | solution.py:190
  222.6 1.0 multiply_convert_fusion.1
  223.6 1.2 convolution_convert_fusion.6
  224.9 3.4 convolution_convert_fusion.1
  228.4 2.2 multiply_convert_fusion
  230.5 0.9 copy-done.26
  231.4 1.9 convolution_convert_fusion
  233.4 3.2 convolution_convert_fusion.3
  238.7 1.3 add_convert_fusion
  241.0 4.8 reduce-scatter.25.cloned.1.call-done
  245.8 1.6 copy.48
  247.7 14.3 %all-reduce.12 = (f32[192]{0:T(256)}, f32[192]{0:T(256)}, f32[768]{0:T(1024)}) all-reduce(f32[192]{0:T(256)S(1)} %reduce_sum.200, f32[192]{0:T(256)S(1)} %reduce_sum.202, f32[768]{0:T(1024)S(1)} %copy-done.51), channel_id=1, replica_groups=mesh['clip'=4,'ctx'=2,'tp'=4] {'clip','ctx'}, use_global_device_ids=true, to_apply=%region_26.0 | all-reduce | flops 1152 | bytes 9216 | tf_op jit(solution)/shard_map/psum | solution.py:296
  262.0 7.6 %reduce-scatter.15.cloned.1.call-done = bf16[192,192]{1,0:T(8,128)(2,1)} async-done(((bf16[768,192]{1,0:T(8,128)(2,1)}), bf16[192,192]{1,0:T(8,128)(2,1)}) %reduce-scatter.15.cloned.1.call-update) | async-done | bytes 73744 | tf_op jit(solution)/shard_map/reduce_scatter | solution.py:217
  269.6 23.4 %reduce-scatter.19.cloned.1.call-done = bf16[192,192]{1,0:T(8,128)(2,1)} async-done(((bf16[768,192]{1,0:T(8,128)(2,1)}), bf16[192,192]{1,0:T(8,128)(2,1)}) %reduce-scatter.19.cloned.1.call-update) | async-done | bytes 73744 | tf_op jit(solution)/shard_map/reduce_scatter | solution.py:223
  292.9 23.9 %reduce-scatter.17.cloned.1.call-done = bf16[192,192]{1,0:T(8,128)(2,1)} async-done(((bf16[768,192]{1,0:T(8,128)(2,1)}), bf16[192,192]{1,0:T(8,128)(2,1)}) %reduce-scatter.17.cloned.1.call-update) | async-done | bytes 73744 | tf_op jit(solution)/shard_map/reduce_scatter | solution.py:220
  316.9 28.3 %reduce-scatter.21.cloned.1.call-done = bf16[192,768]{1,0:T(8,128)(2,1)} async-done(((bf16[768,768]{1,0:T(8,128)(2,1)}), bf16[192,768]{1,0:T(8,128)(2,1)}) %reduce-scatter.21.cloned.1.call-update) | async-done | bytes 294928 | tf_op jit(solution)/shard_map/reduce_scatter | solution.py:238
  345.2 28.9 %reduce-scatter.23.cloned.1.call-done = bf16[768,192]{0,1:T(8,128)(2,1)} async-done(((bf16[768,768]{0,1:T(8,128)(2,1)}), bf16[768,192]{0,1:T(8,128)(2,1)}) %reduce-scatter.23.cloned.1.call-update) | async-done | bytes 294928 | tf_op jit(solution)/shard_map/reduce_scatter | solution.py:241
  374.2 72.5 %all-reduce.27.cloned.1.call-done = (bf16[512,768]{1,0:T(8,128)(2,1)}, bf16[512,768]{1,0:T(8,128)(2,1)}) async-done(((bf16[512,768]{1,0:T(8,128)(2,1)}, bf16[512,768]{1,0:T(8,128)(2,1)}), (bf16[512,768]{1,0:T(8,128)(2,1)}, bf16[512,768]{1,0:T(8,128)(2,1)})) %all-reduce.27.cloned.1.call-update) | async-done | bytes 1572880 | tf_op jit(solution)/shard_map/psum | solution.py:143
  446.7 2.0 fusion.35
  448.6 1.3 reduce_sum.198
  449.9 10.4 %all-reduce.14 = (bf16[768]{0:T(1024)(128)(2,1)S(1)}, bf16[768]{0:T(1024)(128)(2,1)S(1)}, bf16[768]{0:T(1024)(128)(2,1)S(1)}, bf16[768]{0:T(1024)(128)(2,1)S(1)}...) all-reduce(bf16[768]{0:T(1024)(128)(2,1)S(1)} %dynamic-update-slice, ...), channel_id=1, replica_groups=mesh['clip'=4,'ctx'=2,'tp'=4] {'clip'}, use_global_device_ids=true, to_apply=%add.5 | all-reduce | flops 5376 | bytes 21504
  460.8 5.0 all-reduce.16
  469.2 3.6 fusion.27
  472.8 15.6 %all-reduce.29.cloned.1.call-done = (bf16[192,192]{1,0:T(8,128)(2,1)}, bf16[192,192]{1,0:T(8,128)(2,1)}, bf16[192,192]{1,0:T(8,128)(2,1)}, bf16[192,192]{1,0:T(8...) async-done(((bf16[192,192]{1,0:T(8,128)(2,1)}, bf16[192,192]{1,0:T(8,128)(2,1)}, bf16[192,192]{1,0:T(8,128)(2,1)}, bf16[192,192]{1,0:T(8,128)(2,1)}, ...) | async-done | bytes 884752 | tf_op jit(solution)/shard_map/psum | solution.py:269
  488.4 1.6 convert_element_type.296
  490.0 1.6 convert_element_type.299
  491.6 1.6 convert_element_type.301
  493.2 1.6 convert_element_type.304
  494.8 1.8 convert_element_type.310
  496.6 0.9 convert_element_type.313
  (207 shorter events, 19.4 us)
Async XLA Ops:
  8.0 4.5 copy-start.54
  8.0 5.8 %copy-start.56 = (bf16[192]{0:T(256)(128)(2,1)S(1)}, bf16[192]{0:T(256)(128)(2,1)}, u32[]{:S(2)}) copy-start(bf16[192]{0:T(256)(128)(2,1)} %param.19) | copy-start | bytes 1156
  8.0 6.0 %copy-start.57 = (bf16[192]{0:T(256)(128)(2,1)S(1)}, bf16[192]{0:T(256)(128)(2,1)}, u32[]{:S(2)}) copy-start(bf16[192]{0:T(256)(128)(2,1)} %param.20) | copy-start | bytes 1156
  8.1 6.2 %copy-start.58 = (bf16[192]{0:T(256)(128)(2,1)S(1)}, bf16[192]{0:T(256)(128)(2,1)}, u32[]{:S(2)}) copy-start(bf16[192]{0:T(256)(128)(2,1)} %param.27) | copy-start | bytes 1156
  8.1 6.5 %copy-start.59 = (bf16[192]{0:T(256)(128)(2,1)S(1)}, bf16[192]{0:T(256)(128)(2,1)}, u32[]{:S(2)}) copy-start(bf16[192]{0:T(256)(128)(2,1)} %param.28) | copy-start | bytes 1156
  8.1 6.7 %copy-start.60 = (bf16[192]{0:T(256)(128)(2,1)S(1)}, bf16[192]{0:T(256)(128)(2,1)}, u32[]{:S(2)}) copy-start(bf16[192]{0:T(256)(128)(2,1)} %param.29) | copy-start | bytes 1156
  8.1 19.5 %copy-start.28 = (bf16[192,192]{1,0:T(8,128)(2,1)S(1)}, bf16[192,192]{1,0:T(8,128)(2,1)}, u32[]{:S(2)}) copy-start(bf16[192,192]{1,0:T(8,128)(2,1)} %param.26) | copy-start | bytes 221188
  8.1 25.8 %copy-start.29 = (bf16[192,192]{1,0:T(8,128)(2,1)S(1)}, bf16[192,192]{1,0:T(8,128)(2,1)}, u32[]{:S(2)}) copy-start(bf16[192,192]{1,0:T(8,128)(2,1)} %param.21) | copy-start | bytes 221188
  8.1 32.3 %copy-start.30 = (bf16[192,192]{1,0:T(8,128)(2,1)S(1)}, bf16[192,192]{1,0:T(8,128)(2,1)}, u32[]{:S(2)}) copy-start(bf16[192,192]{1,0:T(8,128)(2,1)} %param.23) | copy-start | bytes 221188
  8.1 114.0 %all-reduce.23.cloned.1.call-start = ((), (), s32[]{:S(2)}) async-start(), calls=%async_computation.8 | async-start | bytes 1572864 | tf_op jit(solution)/shard_map/psum | solution.py:123
  9.6 37.4 %copy-start.31 = (bf16[192,192]{1,0:T(8,128)(2,1)S(1)}, bf16[192,192]{1,0:T(8,128)(2,1)}, u32[]{:S(2)}) copy-start(bf16[192,192]{1,0:T(8,128)(2,1)} %param.24) | copy-start | bytes 221188
  10.9 42.7 %copy-start.1 = (bf16[512,768]{1,0:T(8,128)(2,1)S(1)}, bf16[512,768]{1,0:T(8,128)(2,1)}, u32[]{:S(2)}) copy-start(bf16[512,768]{1,0:T(8,128)(2,1)} %param.17) | copy-start | bytes 2359300
  10.9 43.0 %copy-start.35 = (f32[512]{0:T(512)}, f32[512]{0:T(512)S(1)}, u32[]{:S(2)}) copy-start(f32[512]{0:T(512)S(1)} %broadcast_multiply_fusion.5) | copy-start | bytes 6148
  12.5 41.4 %copy-start.42 = (f32[512]{0:T(512)}, f32[512]{0:T(512)S(1)}, u32[]{:S(2)}) copy-start(f32[512]{0:T(512)S(1)} %add_rsqrt_fusion.1) | copy-start | bytes 6148
  33.9 41.9 %copy-start.11 = (bf16[192,768]{0,1:T(8,128)(2,1)}, bf16[192,768]{0,1:T(8,128)(2,1)S(1)}, u32[]{:S(2)}) copy-start(bf16[192,768]{0,1:T(8,128)(2,1)S(1)} %all_gather.51) | copy-start | bytes 884740
  40.5 29.2 %copy-start.9 = (bf16[768,192]{1,0:T(8,128)(2,1)}, bf16[768,192]{1,0:T(8,128)(2,1)S(1)}, u32[]{:S(2)}) copy-start(bf16[768,192]{1,0:T(8,128)(2,1)S(1)} %all_gather.50) | copy-start | bytes 884740
  47.0 15.2 %copy-start.7 = (bf16[768,192]{1,0:T(8,128)(2,1)}, bf16[768,192]{1,0:T(8,128)(2,1)S(1)}, u32[]{:S(2)}) copy-start(bf16[768,192]{1,0:T(8,128)(2,1)S(1)} %all_gather.48) | copy-start | bytes 884740
  53.6 8.6 %copy-start.5 = (bf16[768,192]{1,0:T(8,128)(2,1)}, bf16[768,192]{1,0:T(8,128)(2,1)S(1)}, u32[]{:S(2)}) copy-start(bf16[768,192]{1,0:T(8,128)(2,1)S(1)} %all_gather.46) | copy-start | bytes 884740
  69.7 1.5 copy-start.13
  71.2 2.7 copy-start
  75.7 4.6 copy-start.53
  77.7 47.1 %all-gather.3.cloned.1.call-start = ((), (), s32[]{:S(2)}) async-start(), calls=%async_computation.9 | async-start | bytes 1474560 | tf_op jit(solution)/shard_map/all_gather | solution.py:126
  78.3 50.1 %all-gather.5.cloned.1.call-start = ((), (), s32[]{:S(2)}) async-start(), calls=%async_computation.10 | async-start | bytes 1474560 | tf_op jit(solution)/shard_map/all_gather | solution.py:127
  78.9 102.5 %all-reduce.25.cloned.1.call-start = ((), (), s32[]{:S(2)}) async-start(), calls=%async_computation.11 | async-start | bytes 1572864 | tf_op jit(solution)/shard_map/psum | solution.py:152
  122.2 1.5 copy-start.3
  124.8 3.6 copy-start.24
  128.4 8.2 %copy-start.55 = (bf16[768,768]{1,0:T(8,128)(2,1)S(1)}, bf16[768,768]{1,0:T(8,128)(2,1)}, u32[]{:S(2)}) copy-start(bf16[768,768]{1,0:T(8,128)(2,1)} %all-gather.3.cloned.1.call-done) | copy-start | bytes 3538948
  136.5 1.8 copy-start.34
  136.5 44.9 %copy-start.37 = (f32[768]{0:T(1024)S(1)}, f32[768]{0:T(1024)}, u32[]{:S(2)}) copy-start(f32[768]{0:T(1024)} %convert_element_type.261) | copy-start | bytes 9220
  136.6 44.9 %copy-start.40 = (f32[512]{0:T(512)S(1)}, f32[512]{0:T(512)}, u32[]{:S(2)}) copy-start(f32[512]{0:T(512)} %copy-done.39) | copy-start | bytes 6148
  136.6 44.9 %copy-start.44 = (f32[512]{0:T(512)S(1)}, f32[512]{0:T(512)}, u32[]{:S(2)}) copy-start(f32[512]{0:T(512)} %add_rsqrt_fusion) | copy-start | bytes 6148
  138.3 73.0 %reduce-scatter.13.cloned.1.call-start = ((), (), s32[]{:S(2)}) async-start(), calls=%async_computation.13 | async-start | bytes 589824 | tf_op jit(solution)/shard_map/reduce_scatter | solution.py:193
  181.4 2.7 copy-start.15
  184.2 3.3 copy-start.12
  187.5 1.7 copy-start.32
  188.0 1.2 copy-start.16
  194.0 28.6 %reduce-scatter.11.cloned.1.call-start = ((), (), s32[]{:S(2)}) async-start(), calls=%async_computation.12 | async-start | bytes 589824 | tf_op jit(solution)/shard_map/reduce_scatter | solution.py:190
  194.0 6.3 %copy-start.21 = (bf16[512,192]{0,1:T(8,128)(2,1)S(1)}, bf16[512,192]{0,1:T(8,128)(2,1)}, u32[]{:S(2)}) copy-start(bf16[512,192]{0,1:T(8,128)(2,1)} %copy-done.20) | copy-start | bytes 589828
  198.7 1.6 copy-start.2
  202.1 4.0 copy-start.14
  202.1 43.7 %reduce-scatter.25.cloned.1.call-start = ((), (), s32[]{:S(2)}) async-start(), calls=%async_computation.19 | async-start | bytes 491520
  206.1 63.5 %reduce-scatter.15.cloned.1.call-start = ((), (), s32[]{:S(2)}) async-start(), calls=%async_computation.14 | async-start | bytes 491520 | tf_op jit(solution)/shard_map/reduce_scatter | solution.py:217
  211.3 81.7 %reduce-scatter.19.cloned.1.call-start = ((), (), s32[]{:S(2)}) async-start(), calls=%async_computation.16 | async-start | bytes 491520 | tf_op jit(solution)/shard_map/reduce_scatter | solution.py:223
  213.5 11.4 %copy-start.38 = (f32[768]{0:T(1024)S(1)}, f32[768]{0:T(1024)}, u32[]{:S(2)}) copy-start(f32[768]{0:T(1024)} %convert_element_type.261) | copy-start | bytes 9220
  213.5 11.4 %copy-start.41 = (f32[512]{0:T(512)S(1)}, f32[512]{0:T(512)}, u32[]{:S(2)}) copy-start(f32[512]{0:T(512)} %copy-done.39) | copy-start | bytes 6148
  213.5 11.4 %copy-start.45 = (f32[512]{0:T(512)S(1)}, f32[512]{0:T(512)}, u32[]{:S(2)}) copy-start(f32[512]{0:T(512)} %add_rsqrt_fusion) | copy-start | bytes 6148
  213.5 11.4 %copy-start.52 = (f32[768]{0:T(1024)S(1)}, f32[768]{0:T(1024)}, u32[]{:S(2)}) copy-start(f32[768]{0:T(1024)} %convert_element_type.262) | copy-start | bytes 9220
  213.5 103.4 %reduce-scatter.17.cloned.1.call-start = ((), (), s32[]{:S(2)}) async-start(), calls=%async_computation.15 | async-start | bytes 491520 | tf_op jit(solution)/shard_map/reduce_scatter | solution.py:220
  224.8 120.4 %reduce-scatter.21.cloned.1.call-start = ((), (), s32[]{:S(2)}) async-start(), calls=%async_computation.17 | async-start | bytes 1474560 | tf_op jit(solution)/shard_map/reduce_scatter | solution.py:238
  228.3 145.8 %reduce-scatter.23.cloned.1.call-start = ((), (), s32[]{:S(2)}) async-start(), calls=%async_computation.18 | async-start | bytes 1474560 | tf_op jit(solution)/shard_map/reduce_scatter | solution.py:241
  228.4 3.1 copy-start.25
  233.3 3.3 copy-start.10
  233.3 3.3 copy-start.18
  233.3 213.3 %all-reduce.27.cloned.1.call-start = ((), (), s32[]{:S(2)}) async-start(), calls=%async_computation.20 | async-start | bytes 3145728 | tf_op jit(solution)/shard_map/psum | solution.py:143
  240.0 7.7 %copy-start.51 = (f32[768]{0:T(1024)S(1)}, f32[768]{0:T(1024)}, u32[]{:S(2)}) copy-start(f32[768]{0:T(1024)} %get-tuple-element.52) | copy-start | bytes 9220
  240.0 206.7 %copy-start.36 = (f32[512]{0:T(512)S(1)}, f32[512]{0:T(512)}, u32[]{:S(2)}) copy-start(f32[512]{0:T(512)} %copy-done.35) | copy-start | bytes 6148
  240.0 206.7 %copy-start.43 = (f32[512]{0:T(512)S(1)}, f32[512]{0:T(512)}, u32[]{:S(2)}) copy-start(f32[512]{0:T(512)} %copy-done.42) | copy-start | bytes 6148
  240.0 248.4 %all-reduce.29.cloned.1.call-start = ((), (), s32[]{:S(2)}) async-start(), calls=%async_computation.21 | async-start | bytes 1966080 | tf_op jit(solution)/shard_map/psum | solution.py:269
  374.1 75.8 %copy-start.46 = (bf16[768]{0:T(1024)(128)(2,1)S(1)}, bf16[768]{0:T(1024)(128)(2,1)}, u32[]{:S(2)}) copy-start(bf16[768]{0:T(1024)(128)(2,1)} %get-tuple-element.55) | copy-start | bytes 4612
  374.1 75.8 %copy-start.47 = (bf16[768]{0:T(1024)(128)(2,1)S(1)}, bf16[768]{0:T(1024)(128)(2,1)}, u32[]{:S(2)}) copy-start(bf16[768]{0:T(1024)(128)(2,1)} %get-tuple-element.59) | copy-start | bytes 4612
  374.1 75.8 %copy-start.48 = (bf16[768]{0:T(1024)(128)(2,1)S(1)}, bf16[768]{0:T(1024)(128)(2,1)}, u32[]{:S(2)}) copy-start(bf16[768]{0:T(1024)(128)(2,1)} %get-tuple-element.60) | copy-start | bytes 4612
  374.1 75.8 %copy-start.50 = (bf16[768]{0:T(1024)(128)(2,1)S(1)}, bf16[768]{0:T(1024)(128)(2,1)}, u32[]{:S(2)}) copy-start(bf16[768]{0:T(1024)(128)(2,1)} %get-tuple-element.17) | copy-start | bytes 4612
  374.1 95.1 %copy-start.4 = (bf16[512,768]{1,0:T(8,128)(2,1)S(1)}, bf16[512,768]{1,0:T(8,128)(2,1)}, u32[]{:S(2)}) copy-start(bf16[512,768]{1,0:T(8,128)(2,1)} %all-reduce.23.cloned.1.call-done) | copy-start | bytes 2359300
  488.4 8.2 %copy-start.27 = (bf16[768,192]{0,1:T(8,128)(2,1)S(1)}, bf16[768,192]{0,1:T(8,128)(2,1)}, u32[]{:S(2)}) copy-start(bf16[768,192]{0,1:T(8,128)(2,1)} %get-tuple-element.51) | copy-start | bytes 884740
  (13 other events, 11.1 us)
Sparse Core Ops, SparseCore 0:
  77.8 44.2 all-reduce.22
  138.4 42.9 all-reduce.24
  194.1 12.4 reduce-scatter.12
  209.3 13.2 reduce-scatter.10
  225.0 20.8 reduce-scatter.24
  248.7 20.7 reduce-scatter.14
  272.1 20.8 reduce-scatter.18
  296.0 20.8 reduce-scatter.16
  319.5 25.7 reduce-scatter.20
  348.4 25.7 reduce-scatter.22
  377.1 69.4 all-reduce.26
  449.7 38.6 all-reduce.28
Sparse Core Ops, SparseCore 1:
  79.8 17.9 all-gather.2
  99.1 17.4 all-gather.4
where the time goes:
time: 506 us; the launch traced here: 505 us
  waiting for transfers between devices  299 us (59%)
  blocking collectives  83 us (16%)
  matrix products  50 us (10%)
  other arithmetic  39.9 us (8%)
  between operations  17.6 us (3%)
  local copies, waits for them, and re-layouts  14.6 us (3%)
    psum x1, waiting for transfers between devices, shards(): lax.psum(product(act_low, reduce_full).astype(jnp.bfloat16), 'tp')  72.5 us
    psum x1, waiting for transfers between devices, shards(): lax.psum(cols_inner(grad_pre, expand_full).astype(jnp.bfloat16), 'tp')  42.5 us
    psum x1, waiting for transfers between devices, shards(): lax.psum(product(mixed_low, out_full).astype(jnp.bfloat16), 'tp')  41.2 us
    reduce_scatter x1, waiting for transfers between devices, shards(): lax.psum_scatter(grad_reduce.astype(jnp.bfloat16), 'clip', scatter_dimens...  28.9 us
    reduce_scatter x1, waiting for transfers between devices, shards(): lax.psum_scatter(grad_expand.astype(jnp.bfloat16), 'clip', scatter_dimens...  28.3 us
    reduce_scatter x1, waiting for transfers between devices, shards(): lax.psum_scatter(grad_key_weight.astype(jnp.bfloat16), 'clip', scatter_di...  23.9 us
    reduce_scatter x1, waiting for transfers between devices, shards(): lax.psum_scatter(grad_value_weight.astype(jnp.bfloat16), 'clip', scatter_...  23.4 us
    unnamed x2, blocking collectives  23.1 us
  transfers between devices with their start and end apart: 14, of which 11 were waited for; matrix products, arithmetic and copies ran while one was open for 11% of the time, Pallas kernels for 0%

commit v1 on v0

v1 whole, which is shorter than its diff:
```python
import functools
import itertools

import jax
import jax.numpy as jnp
from jax import lax
from jax.experimental import pallas as pl
from jax.experimental.pallas import tpu as pltpu
from jax.sharding import PartitionSpec as P

DH = 64


def center_rows(matrix):
    row_mean = jnp.mean(matrix, axis=-1, keepdims=True)
    centred = matrix - row_mean
    factor = lax.rsqrt(jnp.mean(centred * centred, axis=-1, keepdims=True) + 1e-05)
    return (centred * factor, factor)


def norm_back(grad_norm, normed, factor, gain):
    grad_hat = grad_norm * gain
    inner = jnp.mean(grad_hat, axis=-1, keepdims=True)
    cross = jnp.mean(grad_hat * normed, axis=-1, keepdims=True)
    return factor * (grad_hat - inner - normed * cross)


def product(left, right):
    return jnp.dot(left, right, preferred_element_type=jnp.float32)


def rows_inner(left, right):
    return lax.dot_general(
        left, right, (((0,), (0,)), ((), ())), preferred_element_type=jnp.float32
    )


def cols_inner(left, right):
    return lax.dot_general(
        left, right, (((1,), (1,)), ((), ())), preferred_element_type=jnp.float32
    )


def score_block(query_heads, key_heads, value_heads, grad_heads, log_total, row_delta, score_scale):
    scores = (
        jnp.einsum("qhd,khd->qhk", query_heads, key_heads, preferred_element_type=jnp.float32)
        * score_scale
    )
    weights = jnp.exp(scores - log_total[..., None])
    grad_weights = jnp.einsum(
        "qhd,khd->qhk", grad_heads, value_heads, preferred_element_type=jnp.float32
    )
    grad_scores = (weights * (grad_weights - row_delta[..., None])).astype(jnp.bfloat16)
    return (weights.astype(jnp.bfloat16), grad_scores)


F32 = jnp.float32
BF16 = jnp.bfloat16


def offsets(sizes):
    return [o for o in itertools.product(*(range(s) for s in sizes)) if any(o)]


def group_place(axes, sizes, offset):
    index = 0
    place = {}
    for axis, size, step in zip(axes, sizes, offset):
        at = lax.rem(lax.axis_index(axis) + step, size)
        place[axis] = at
        index = index * size + at
    return place, index


def rows_at(index, rows):
    return pl.ds(pl.multiple_of(index * rows, rows), rows)


def send(src, dst, sems, slot, place):
    copy = pltpu.make_async_remote_copy(
        src_ref=src,
        dst_ref=dst,
        send_sem=sems.at[0, slot],
        recv_sem=sems.at[1, slot],
        device_id=place,
        device_id_type=pl.DeviceIdType.MESH,
    )
    copy.start()
    return copy


def finish(copies):
    for copy in copies:
        copy.wait_send()


def spread(src, dst, rows, axes, sizes, sems):
    _, mine = group_place(axes, sizes, (0,) * len(axes))
    copies = []
    for slot, offset in enumerate(offsets(sizes)):
        place, _ = group_place(axes, sizes, offset)
        copies.append(send(src, dst.at[rows_at(mine, rows)], sems, slot, place))
    return mine, copies


def deal(src, landing, rows, axes, sizes, sems):
    copies = []
    for slot, offset in enumerate(offsets(sizes)):
        place, theirs = group_place(axes, sizes, offset)
        copies.append(send(src.at[rows_at(theirs, rows)], landing.at[slot], sems, slot, place))
    _, mine = group_place(axes, sizes, (0,) * len(axes))
    return mine, copies


def gather_steps(axes, sizes, src, out, sems):
    rows = src.shape[0]
    mine, copies = spread(src, out, rows, axes, sizes, sems)
    out[rows_at(mine, rows), :] = src[...]
    yield
    for copy in copies:
        copy.wait_recv()
    finish(copies)


def scatter_steps(axes, sizes, src, out, landing, sems):
    rows = out.shape[0]
    mine, copies = deal(src, landing, rows, axes, sizes, sems)
    yield
    total = src[rows_at(mine, rows), :].astype(F32)
    for slot, copy in enumerate(copies):
        copy.wait_recv()
        total = total + landing[slot].astype(F32)
    out[...] = total.astype(out.dtype)
    finish(copies)


def reduce_steps(axes, sizes, src, out, landing, sems, back_sems):
    rows = landing.shape[1]
    mine, copies = deal(src, landing, rows, axes, sizes, sems)
    yield
    total = src[rows_at(mine, rows), :].astype(F32)
    for slot, copy in enumerate(copies):
        copy.wait_recv()
        total = total + landing[slot].astype(F32)
    block = rows_at(mine, rows)
    out[block, :] = total.astype(out.dtype)
    _, backs = spread(out.at[block], out, rows, axes, sizes, back_sems)
    yield
    for copy in backs:
        copy.wait_recv()
    finish(copies)
    finish(backs)


def sum_blocks(held, rows, count):
    total = held[0:rows, :].astype(F32)
    for index in range(1, count):
        total = total + held[index * rows : (index + 1) * rows, :].astype(F32)
    return total


def share_steps(axes, sizes, src, out, held, sems):
    rows = src.shape[0]
    mine, copies = spread(src, held, rows, axes, sizes, sems)
    held[rows_at(mine, rows), :] = src[...]
    yield
    for copy in copies:
        copy.wait_recv()
    out[...] = sum_blocks(held, rows, len(copies) + 1).astype(out.dtype)
    finish(copies)


def both_steps(axes, sizes, more_axes, more_sizes, src, out, landing, part, held, sems, more_sems):
    rows = out.shape[0]
    mine, copies = deal(src, landing, rows, axes, sizes, sems)
    yield
    total = src[rows_at(mine, rows), :].astype(F32)
    for slot, copy in enumerate(copies):
        copy.wait_recv()
        total = total + landing[slot].astype(F32)
    part[...] = total.astype(part.dtype)
    at, mores = spread(part, held, rows, more_axes, more_sizes, more_sems)
    held[rows_at(at, rows), :] = part[...]
    yield
    for copy in mores:
        copy.wait_recv()
    out[...] = sum_blocks(held, rows, len(mores) + 1).astype(out.dtype)
    finish(copies)
    finish(mores)


def plan_of(kind, axes, sizes, more, array, out_type):
    rows, cols = array.shape
    count = 1
    for size in sizes:
        count *= size
    peers = count - 1
    pair = pltpu.SemaphoreType.DMA((2, peers))
    if kind == "gather":
        return (count * rows, cols), [pair], functools.partial(gather_steps, axes, sizes)
    if kind == "share":
        held = pltpu.VMEM((count * rows, cols), array.dtype)
        return (rows, cols), [held, pair], functools.partial(share_steps, axes, sizes)
    block = rows // count
    landing = pltpu.VMEM((peers, block, cols), array.dtype)
    if kind == "scatter":
        return (block, cols), [landing, pair], functools.partial(scatter_steps, axes, sizes)
    if kind == "reduce":
        return (
            (rows, cols),
            [landing, pair, pair],
            functools.partial(reduce_steps, axes, sizes),
        )
    more_axes, more_sizes = more
    more_count = 1
    for size in more_sizes:
        more_count *= size
    return (
        (block, cols),
        [
            landing,
            pltpu.VMEM((block, cols), array.dtype),
            pltpu.VMEM((more_count * block, cols), array.dtype),
            pair,
            pltpu.SemaphoreType.DMA((2, more_count - 1)),
        ],
        functools.partial(both_steps, axes, sizes, more_axes, more_sizes),
    )


def transfers(collective_id, name, jobs):
    def sized(axes):
        return tuple(lax.axis_size(axis) for axis in axes)

    plans = []
    groups = []
    for job in jobs:
        kind, axes, array, out_type = job[:4]
        more = (job[4], sized(job[4])) if len(job) > 4 else None
        plans.append(plan_of(kind, axes, sized(axes), more, array, out_type))
        for group in (axes,) + ((job[4],) if len(job) > 4 else ()):
            if group not in groups:
                groups.append(group)
    places = {}
    for group in groups:
        for offset in offsets(sized(group)):
            key = tuple(sorted((a, o) for a, o in zip(group, offset) if o))
            places.setdefault(key, (group, offset))
    count = len(jobs)

    def kernel(*refs):
        sources, outs = refs[:count], refs[count : 2 * count]
        scratch = list(refs[2 * count :])
        barrier = pltpu.get_barrier_semaphore()
        for group, offset in places.values():
            place, _ = group_place(group, sized(group), offset)
            pl.semaphore_signal(
                barrier, inc=1, device_id=place, device_id_type=pl.DeviceIdType.MESH
            )
        pl.semaphore_wait(barrier, len(places))
        running = []
        for source, out, (_, needs, steps) in zip(sources, outs, plans):
            mine, scratch = scratch[: len(needs)], scratch[len(needs) :]
            running.append(steps(source, out, *mine))
        while running:
            running = [step for step in running if next(step, "end") != "end"]

    whole = pl.BlockSpec(memory_space=pltpu.VMEM)
    return pl.pallas_call(
        kernel,
        name=name,
        out_shape=[
            jax.ShapeDtypeStruct(plan[0], job[3]) for plan, job in zip(plans, jobs)
        ],
        in_specs=[whole] * count,
        out_specs=[whole] * count,
        scratch_shapes=[need for plan in plans for need in plan[1]],
        compiler_params=pltpu.CompilerParams(
            collective_id=collective_id,
            has_side_effects=True,
            vmem_limit_bytes=56 * 1024 * 1024,
        ),
    )(*[job[2] for job in jobs])


def pack_vectors(vectors):
    flat = jnp.concatenate(vectors)
    width = -(-flat.shape[0] // (8 * 128)) * 128
    return jnp.pad(flat, (0, 8 * width - flat.shape[0])).reshape(8, width)


def unpack_vectors(packed, sizes):
    flat = packed.reshape(-1)
    out = []
    at = 0
    for size in sizes:
        out.append(flat[at : at + size])
        at += size
    return out


def shards(
    frames,
    cotangent,
    first_gain,
    first_shift,
    query_weight,
    query_bias,
    key_weight,
    value_weight,
    value_bias,
    out_weight,
    out_bias,
    second_gain,
    second_shift,
    expand_weight,
    expand_bias,
    reduce_weight,
    reduce_bias,
):
    row_count, width = frames.shape
    local_width = query_weight.shape[1]
    head_count = local_width // DH
    score_scale = DH ** (-0.5)
    share = first_gain.shape[0]
    hidden_width = expand_weight.shape[1]
    clips = lax.axis_size("clip")
    clip_at = lax.axis_index("clip") * share
    wide = -(-share // 128) * 128
    vectors = jnp.pad(
        jnp.stack([first_gain, first_shift, out_bias, second_gain, second_shift, reduce_bias]),
        ((0, 10), (0, wide - share)),
    )
    attn_weights = jnp.concatenate([query_weight, key_weight, value_weight, out_weight.T], axis=1)
    attn_full, vectors_full, frames_all = transfers(
        1,
        "gather_first",
        [
            ("gather", ("clip",), attn_weights, BF16),
            ("gather", ("clip",), vectors, BF16),
            ("gather", ("ctx",), frames, BF16),
        ],
    )
    vectors_full = vectors_full.reshape(clips, 16, wide)[:, :6, :share]
    vectors_full = vectors_full.transpose(1, 0, 2).reshape(6, width).astype(F32)
    gain_first, shift_first, out_shift, gain_second, shift_second, reduce_shift = [
        vectors_full[i] for i in range(6)
    ]
    qkv_full = attn_full[:, : 3 * local_width]
    kv_full = attn_full[:, local_width : 3 * local_width]
    query_full = attn_full[:, :local_width]
    out_full_t = attn_full[:, 3 * local_width :]
    inputs = frames.astype(F32)
    normed_one, factor_one = center_rows(inputs)
    first_norm = (normed_one * gain_first + shift_first).astype(BF16)
    queries = (product(first_norm, query_full) + query_bias.astype(F32)).astype(BF16)
    normed_all, _ = center_rows(frames_all.astype(F32))
    norm_all = (normed_all * gain_first + shift_first).astype(BF16)
    kv_bias = jnp.concatenate([jnp.zeros_like(value_bias), value_bias]).astype(F32)
    kv_rows = (product(norm_all, kv_full) + kv_bias).astype(BF16)
    length = kv_rows.shape[0]
    query_heads = queries.reshape(row_count, head_count, DH)
    key_heads = kv_rows[:, :local_width].reshape(length, head_count, DH)
    value_heads = kv_rows[:, local_width:].reshape(length, head_count, DH)
    scores = (
        jnp.einsum("qhd,khd->qhk", query_heads, key_heads, preferred_element_type=F32)
        * score_scale
    )
    run_max = jnp.max(scores, axis=-1)
    weights = jnp.exp(scores - run_max[..., None])
    run_sum = jnp.sum(weights, axis=-1)
    run_acc = jnp.einsum(
        "qhk,khd->qhd", weights.astype(BF16), value_heads, preferred_element_type=F32
    )
    mixed_full = run_acc / run_sum[..., None]
    log_total = run_max + jnp.log(run_sum)
    mixed_low = mixed_full.reshape(row_count, local_width).astype(BF16)
    attn_sum, expand_full, reduce_full_t = transfers(
        2,
        "attn_sum",
        [
            ("reduce", ("tp",), cols_inner(mixed_low, out_full_t).astype(BF16), BF16),
            ("gather", ("clip",), expand_weight, BF16),
            ("gather", ("clip",), reduce_weight.T, BF16),
        ],
    )
    hidden = inputs + attn_sum.astype(F32) + out_shift
    normed_two, factor_two = center_rows(hidden)
    second_norm = (normed_two * gain_second + shift_second).astype(BF16)
    pre_act = product(second_norm, expand_full) + expand_bias.astype(F32)

    def gelu_exact(argument):
        return jax.nn.gelu(argument, approximate=False)

    activated, gelu_pull = jax.vjp(gelu_exact, pre_act)
    act_low = activated.astype(BF16)
    grad_act = product(cotangent, reduce_full_t)
    grad_pre = gelu_pull(grad_act)[0].astype(BF16)
    second_terms = cols_inner(grad_pre, expand_full).astype(BF16)
    grad_expand = rows_inner(second_norm, grad_pre).astype(BF16)
    grad_reduce_t = rows_inner(cotangent, act_low).astype(BF16)
    grad_second, share_expand, share_reduce_t = transfers(
        3,
        "grad_second",
        [
            ("reduce", ("tp",), second_terms, BF16),
            ("scatter", ("clip",), grad_expand, BF16),
            ("scatter", ("clip",), grad_reduce_t, BF16),
        ],
    )
    act_late, grad_second = lax.optimization_barrier((act_low, grad_second))
    mlp_sum = lax.psum(cols_inner(act_late, reduce_full_t).astype(BF16), "tp").astype(F32)
    layer_out = (hidden + mlp_sum + reduce_shift).astype(BF16)
    grad_out = cotangent.astype(F32)
    grad_second = grad_second.astype(F32)
    grad_hidden = grad_out + norm_back(grad_second, normed_two, factor_two, gain_second)
    grad_attn = grad_hidden.astype(BF16)
    grad_out_weight_t = rows_inner(grad_attn, mixed_low).astype(BF16)
    grad_mixed = product(grad_attn, out_full_t).astype(BF16)
    grad_heads = grad_mixed.reshape(row_count, head_count, DH)
    row_delta = jnp.sum(grad_heads.astype(F32) * mixed_full, axis=-1)
    weights_low, grad_scores = score_block(
        query_heads, key_heads, value_heads, grad_heads, log_total, row_delta, score_scale
    )
    grad_query = jnp.einsum("qhk,khd->qhd", grad_scores, key_heads, preferred_element_type=F32)
    key_term = jnp.einsum("qhk,qhd->khd", grad_scores, query_heads, preferred_element_type=F32)
    value_term = jnp.einsum("qhk,qhd->khd", weights_low, grad_heads, preferred_element_type=F32)
    kv_terms = jnp.concatenate(
        [
            (key_term * score_scale).reshape(length, local_width),
            value_term.reshape(length, local_width),
        ],
        axis=1,
    ).astype(BF16)
    (grad_kv_low,) = transfers(4, "grad_kv", [("scatter", ("ctx",), kv_terms, BF16)])
    grad_q_low = (grad_query * score_scale).reshape(row_count, local_width).astype(BF16)
    grad_qkv = jnp.concatenate([grad_q_low, grad_kv_low], axis=1)
    first_terms = cols_inner(grad_qkv, qkv_full).astype(BF16)
    grad_attn_weights = jnp.concatenate(
        [rows_inner(first_norm, grad_qkv).astype(BF16), grad_out_weight_t], axis=1
    )
    qkv_bias = jnp.sum(grad_qkv.astype(F32), axis=0)
    early = [
        jnp.sum(grad_out, axis=0),
        jnp.sum(grad_second * normed_two, axis=0),
        jnp.sum(grad_second, axis=0),
        jnp.sum(grad_attn.astype(F32), axis=0),
        jnp.sum(grad_pre.astype(F32), axis=0),
        qkv_bias[:local_width],
        qkv_bias[2 * local_width :],
    ]
    grad_first, sum_attn, sum_expand, sum_reduce_t, early_sum = transfers(
        5,
        "grad_first",
        [
            ("reduce", ("tp",), first_terms, BF16),
            ("both", ("clip",), grad_attn_weights, F32, ("ctx",)),
            ("share", ("ctx",), share_expand, F32),
            ("share", ("ctx",), share_reduce_t, F32),
            ("share", ("clip", "ctx"), pack_vectors(early), F32),
        ],
    )
    grad_first = grad_first.astype(F32)
    late = [jnp.sum(grad_first * normed_one, axis=0), jnp.sum(grad_first, axis=0)]
    (late_sum,) = transfers(
        6, "gain_sums", [("share", ("clip", "ctx"), pack_vectors(late), F32)]
    )
    frames_grad = grad_hidden + norm_back(grad_first, normed_one, factor_one, gain_first)

    def mine(vector):
        return lax.dynamic_slice(vector, (clip_at,), (share,))

    sums = unpack_vectors(
        early_sum, [width] * 4 + [hidden_width, local_width, local_width]
    )
    gain_one, shift_one = unpack_vectors(late_sum, [width] * 2)
    return (
        layer_out,
        frames_grad,
        mine(gain_one),
        mine(shift_one),
        sum_attn[:, :local_width],
        sums[5],
        sum_attn[:, local_width : 2 * local_width],
        sum_attn[:, 2 * local_width : 3 * local_width],
        sums[6],
        sum_attn[:, 3 * local_width :].T,
        mine(sums[3]),
        mine(sums[1]),
        mine(sums[2]),
        sum_expand,
        sums[4],
        sum_reduce_t.T,
        mine(sums[0]),
    )


def solution(mesh):
    placed = (
        P(("clip", "ctx"), None),
        P(("clip", "ctx"), None),
        P("clip"),
        P("clip"),
        P("clip", "tp"),
        P("tp"),
        P("clip", "tp"),
        P("clip", "tp"),
        P("tp"),
        P("tp", "clip"),
        P("clip"),
        P("clip"),
        P("clip"),
        P("clip", "tp"),
        P("tp"),
        P("tp", "clip"),
        P("clip"),
    )
    return jax.shard_map(
        shards,
        mesh=mesh,
        in_specs=placed,
        out_specs=(
            P(("clip", "ctx"), None),
            P(("clip", "ctx"), None),
            P("clip"),
            P("clip"),
            P("clip", "tp"),
            P("tp"),
            P("clip", "tp"),
            P("clip", "tp"),
            P("tp"),
            P("tp", "clip"),
            P("clip"),
            P("clip"),
            P("clip"),
            P("clip", "tp"),
            P("tp"),
            P("tp", "clip"),
            P("clip"),
        ),
        check_vma=False,
    )
```

time: 506 us -> 302 us (0.60)
  waiting for transfers between devices: 299 us -> 42.5 us
  Pallas kernels: 0 us -> 162 us
  blocking collectives: 83 us -> 0 us
  matrix products: 50 us -> 31.3 us
  other arithmetic: 39.9 us -> 24.4 us
  local copies, waits for them, and re-layouts: 14.6 us -> 22.9 us
    pallas_call x0 -> x6, Pallas kernels: none -> 162 us  [transfers(): pl.pallas_call(kernel, name=name, out_shape=[jax.ShapeDtypeStruct(plan[0]...]
    psum x4 -> x1, waiting for transfers between devices: 172 us -> 42.5 us  [shards(): lax.psum(cols_inner(act_late, reduce_full_t).astype(BF16), 'tp').astype(F32)]
    reduce_scatter x7 -> x0, waiting for transfers between devices: 121 us -> none  [the longest x1 28.9 us: shards(): lax.psum_scatter(grad_reduce.astype(jnp.bfloat16), 'clip', scatter_dimens...]
    all_gather x6 -> x0, blocking collectives: 40.7 us -> none  [the longest x1 7.83 us: shards(): lax.all_gather(value_rows, 'ctx', axis=0, tiled=True)]
    unnamed x2 -> x0, blocking collectives: 23.1 us -> none
    psum x2 -> x0, blocking collectives: 19.3 us -> none  [the longest x1 14.3 us: shards(): lax.psum((grad_query_bias, grad_value_bias, grad_expand_bias), ('clip', '...]
    convert_element_type x24 -> x4, other arithmetic: 19.1 us -> 2.23 us  [the longest x1 0.84 us: shards(): vectors_full = vectors_full.transpose(1, 0, 2).reshape(6, width).astype(F32)]
    unnamed x148 -> x62, local copies, waits for them, and re-layouts: 14.4 us -> 6.03 us
  transfers between devices with their start and end apart: 14 -> 1, of which waited for: 11 -> 1; matrix products, arithmetic and copies ran while one was open for 11% -> 1% of each run, Pallas kernels for 0% -> 0%
where the time goes in v1:
time: 302 us; the launch traced here: 298 us
  Pallas kernels  162 us (54%)
  waiting for transfers between devices  42.5 us (14%)
  matrix products  31.3 us (10%)
  other arithmetic  24.4 us (8%)
  local copies, waits for them, and re-layouts  22.9 us (8%)
  between operations  14.6 us (5%)
    pallas_call x6, Pallas kernels, transfers(): pl.pallas_call(kernel, name=name, out_shape=[jax.ShapeDtypeStruct(plan[0]...  162 us
    psum x1, waiting for transfers between devices, shards(): lax.psum(cols_inner(act_late, reduce_full_t).astype(BF16), 'tp').astype(F32)  42.5 us
    dot_general x5, matrix products, product(): return jnp.dot(left, right, preferred_element_type=jnp.float32)  9.08 us
    dot_general x4, matrix products, cols_inner(): lax.dot_general(left, right, (((1,), (1,)), ((), ())), preferred_element_...  7.63 us
    dot_general x4, matrix products, rows_inner(): lax.dot_general(left, right, (((0,), (0,)), ((), ())), preferred_element_...  6.27 us
  transfers between devices with their start and end apart: 1, of which 1 were waited for; matrix products, arithmetic and copies ran while one was open for 1% of the time, Pallas kernels for 0%

profile of v1, /device:TPU:0, one launch (start us, length us, event | category | flops | bytes accessed | tf_op | source)
XLA Modules:
  0.0 298.1 jit_solution(14152436782799046629)
XLA Ops:
  7.3 0.8 stack.21
  8.1 0.7 stack.22
  8.7 0.7 convert_element_type.144
  9.4 0.7 stack.23
  10.0 0.7 stack.24
  10.7 0.7 stack.25
  11.3 0.7 stack.26
  12.0 0.7 pad_convert_fusion
  12.7 1.3 convert_reduce_fusion.3
  14.1 1.5 fusion.34
  15.7 0.6 pad.13.refs_1_
  16.3 0.9 pad_maximum_fusion.3.refs_0_
  17.2 25.3 %gather_first.1 = (bf16[768,768]{1,0:T(8,128)(2,1)}, bf16[64,256]{1,0:T(8,128)(2,1)}, bf16[1024,768]{1,0:T(8,128)(2,1)}) custom-call(bf16[192,768]{1,0:T(8,128)(2,1)} %pad_maximum_fusion.3.refs_0_, bf16[16,256]{1,0:T(8,128)(2,1)} %pad.13.refs_1_, bf16[512,768]{1,0:T(8,128)(2,1)} %refs_2_.1), custom_call_target="tpu_custom_call" | custom-call | tf_op jit(solution)/shard_map/gather_first/pallas_call | solution.py:269
  42.5 0.8 convert_bitcast_fusion
  43.8 1.8 convert_reduce_fusion
  46.2 1.3 add_convert_fusion.2
  47.6 1.1 copy-done.1
  49.3 1.0 bitcast_reduce_fusion
  50.4 1.0 fusion.5
  51.4 1.6 copy-done
  53.0 1.9 fusion.96
  54.9 1.4 convolution_convert_fusion.6.refs_0_
  56.4 38.1 %attn_sum.1 = (bf16[512,768]{1,0:T(8,128)(2,1)}, bf16[768,768]{1,0:T(8,128)(2,1)}, bf16[768,768]{1,0:T(8,128)(2,1)}) custom-call(bf16[512,768]{1,0:T(8,128)(2,1)} %convolution_convert_fusion.6.refs_0_, bf16[192,768]{1,0:T(8,128)(2,1)} %refs_1_.1, bf16[192,768]{1,0:T(8,128)(2,1)} %bitcast.119), custom_call_target="tpu_custom_call" | custom-call | tf_op jit(solution)/shard_map/attn_sum/pallas_call | solution.py:269
  94.5 1.6 fusion.78
  96.6 4.4 %multiply_convert_fusion = (bf16[512,768]{1,0:T(8,128)(2,1)S(1)}, f32[512,768]{1,0:T(8,128)S(1)}, f32[512,768]{1,0:T(8,128)S(1)}) fusion(f32[768]{0:T(1024)S(1)} %convert_element_type.152, bf16[768,768]{1,0:T(8,128)(2,1)S(1)} %copy-done.26, f32[768]{0:T(1024)S(1)} %add.153, f32[768]{0:T(1024)S(1)} %mul.191, f32[512]{0:T(512)S(1)} %add_rsqrt_fusion.1, ...), kind=kOutput, calls=%fused_computation.72 | convolution fusion | flops 633470976 | bytes 6701056 | tf_op jit(solution)/shard_map/dot_general | solution.py:29
  101.0 1.2 convert_reduce_fusion.5
  102.2 1.7 convolution_convert_fusion.4.refs_0_
  103.9 2.0 convolution_convert_fusion.1.refs_1_
  106.0 1.9 fusion.61.refs_2_
  107.8 42.1 %grad_second.1 = (bf16[512,768]{1,0:T(8,128)(2,1)}, bf16[192,768]{1,0:T(8,128)(2,1)}, bf16[192,768]{1,0:T(8,128)(2,1)}) custom-call(bf16[512,768]{1,0:T(8,128)(2,1)} %convolution_convert_fusion.4.refs_0_, bf16[768,768]{1,0:T(8,128)(2,1)} %convolution_convert_fusion.1.refs_1_, bf16[768,768]{1,0:T(8,128)(2,1)} %fusion.61.refs_2_), custom_call_target="tpu_custom_call" | custom-call | tf_op jit(solution)/shard_map/grad_second/pallas_call | solution.py:269
  150.0 1.7 convolution_convert_fusion.3
  151.8 2.5 fusion.41
  154.3 42.5 %all-reduce.6.cloned.1.call-done = bf16[512,768]{1,0:T(8,128)(2,1)} async-done(((bf16[512,768]{1,0:T(8,128)(2,1)}), bf16[512,768]{1,0:T(8,128)(2,1)}) %all-reduce.6.cloned.1.call-update) | async-done | bytes 786448 | tf_op jit(solution)/shard_map/psum | solution.py:412
  196.7 3.9 %convert_reduce_fusion.6 = (f32[768]{0:T(1024)S(1)}, f32[512,768]{1,0:T(8,128)S(1)}, bf16[512,768]{1,0:T(8,128)(2,1)}, f32[768]{0:T(1024)S(1)}) fusion(f32[512]{0:T(512)S(1)} %get-tuple-element.144, f32[512]{0:T(512)S(1)} %broadcast_multiply_fusion.5, f32[768]{0:T(1024)S(1)} %add.149, bf16[512,768]{1,0:T(8,128)(2,1)} %get-tuple-element.36, ...), kind=kLoop, calls=%fused_computation.70 | loop fusion | flops 8649216 | bytes 6315008 | tf_op jit(solution)/shard_map/reduce_sum | solution.py:447
  200.7 1.2 convolution_convert_fusion.7
  201.9 1.6 convolution_convert_fusion.8
  203.6 2.0 fusion.65
  205.6 1.8 fusion.1
  207.4 0.6 fusion.71
  208.3 1.1 fusion.64
  210.2 1.2 pad_maximum_fusion.1.refs_0_
  211.4 12.8 %grad_kv.1 = bf16[512,384]{1,0:T(8,128)(2,1)} custom-call(bf16[1024,384]{1,0:T(8,128)(2,1)} %pad_maximum_fusion.1.refs_0_), custom_call_target="tpu_custom_call" | custom-call | tf_op jit(solution)/shard_map/grad_kv/pallas_call | solution.py:269
  224.2 2.8 convolution_convert_fusion.5.refs_0_
  227.3 1.1 convolution_convert_fusion.2
  228.7 0.6 reshape.158.refs_4_
  229.3 0.6 copy.67
  229.9 1.2 pad_maximum_fusion.refs_1_
  231.1 38.0 %grad_first.1 = (bf16[512,768]{1,0:T(8,128)(2,1)}, f32[192,768]{1,0:T(8,128)}, f32[192,768]{1,0:T(8,128)}, f32[192,768]{1,0:T(8,128)}, f32[8,640]{1,0:T(8,128)}) custom-call(bf16[512,768]{1,0:T(8,128)(2,1)} %convolution_convert_fusion.5.refs_0_, bf16[768,768]{1,0:T(8,128)(2,1)} %pad_maximum_fusion.refs_1_, bf16[192,768]{1,0:T(8,128)(2,1)} %get-tuple-element.42.refs_2_, ...), custom_call_target="tpu_custom_call" | custom-call | tf_op jit(solution)/shard_map/grad_first/pallas_call | solution.py:269
  269.2 0.7 reshape.160
  269.9 0.6 fusion.93
  271.1 2.1 fusion.42
  273.8 6.1 %gain_sums.1 = f32[8,256]{1,0:T(8,128)} custom-call(f32[8,256]{1,0:T(8,128)} %reshape.159.refs_0_), custom_call_target="tpu_custom_call" | custom-call | tf_op jit(solution)/shard_map/gain_sums/pallas_call | solution.py:269
  279.9 0.8 fusion.94
  280.7 0.6 dynamic_slice.19
  281.4 0.6 dynamic_slice.18
  282.0 0.6 dynamic_slice.23
  282.6 0.6 dynamic_slice.22
  283.3 0.6 dynamic_slice.21
  283.9 0.6 dynamic_slice.20
  284.5 2.1 slice_bitcast_fusion
  286.7 0.8 copy.69
  287.5 1.7 fusion.33
  289.2 0.8 copy.78
  290.5 0.8 copy.79
  (97 shorter events, 5.9 us)
Async XLA Ops:
  7.2 8.4 %copy-start.24 = (bf16[768]{0:T(1024)(128)(2,1)S(1)}, bf16[768]{0:T(1024)(128)(2,1)}, u32[]{:S(2)}) copy-start(bf16[768]{0:T(1024)(128)(2,1)} %param.31) | copy-start | bytes 4612
  7.2 8.4 %copy-start.20 = (bf16[192,192]{1,0:T(8,128)(2,1)S(1)}, bf16[192,192]{1,0:T(8,128)(2,1)}, u32[]{:S(2)}) copy-start(bf16[192,192]{1,0:T(8,128)(2,1)} %param.26) | copy-start | bytes 221188
  7.2 9.1 %copy-start.21 = (bf16[192,192]{1,0:T(8,128)(2,1)S(1)}, bf16[192,192]{1,0:T(8,128)(2,1)}, u32[]{:S(2)}) copy-start(bf16[192,192]{1,0:T(8,128)(2,1)} %param.24) | copy-start | bytes 221188
  7.2 9.1 %copy-start.22 = (bf16[192,192]{1,0:T(8,128)(2,1)S(1)}, bf16[192,192]{1,0:T(8,128)(2,1)}, u32[]{:S(2)}) copy-start(bf16[192,192]{1,0:T(8,128)(2,1)} %param.23) | copy-start | bytes 221188
  7.2 9.1 %copy-start.23 = (bf16[192,192]{1,0:T(8,128)(2,1)S(1)}, bf16[192,192]{1,0:T(8,128)(2,1)}, u32[]{:S(2)}) copy-start(bf16[192,192]{1,0:T(8,128)(2,1)} %param.21) | copy-start | bytes 221188
  7.2 189.5 %all-reduce.6.cloned.1.call-start = ((), (), s32[]{:S(2)}) async-start(), calls=%async_computation | async-start | bytes 1572864 | tf_op jit(solution)/shard_map/psum | solution.py:412
  42.5 3.1 %copy-start.5 = (bf16[1024,768]{1,0:T(8,128)(2,1)S(1)}, bf16[1024,768]{1,0:T(8,128)(2,1)}, u32[]{:S(2)}) copy-start(bf16[1024,768]{1,0:T(8,128)(2,1)} %get-tuple-element.33) | copy-start | bytes 4718596
  43.8 2.4 copy-start.18
  47.5 1.1 copy-start.1
  48.7 1.7 copy-start.6
  49.3 1.1 copy-start.13
  50.4 2.7 copy-start
  94.5 1.6 copy-start.4
  94.5 2.1 copy-start.26
  96.6 4.4 %copy-start.15 = (bf16[512,768]{1,0:T(8,128)(2,1)S(1)}, bf16[512,768]{1,0:T(8,128)(2,1)}, u32[]{:S(2)}) copy-start(bf16[512,768]{1,0:T(8,128)(2,1)} %param.18) | copy-start | bytes 2359300
  96.6 4.4 %copy-start.25 = (bf16[768,768]{1,0:T(8,128)(2,1)S(1)}, bf16[768,768]{1,0:T(8,128)(2,1)}, u32[]{:S(2)}) copy-start(bf16[768,768]{1,0:T(8,128)(2,1)} %get-tuple-element.38) | copy-start | bytes 3538948
  151.8 51.8 %slice-start = ((s8[6291456]{0:T(1024)(128)(4,1)}), s8[2097152]{0:T(1024)(128)(4,1)S(1)}, s32[]{:S(2)}) async-start(s8[6291456]{0:T(1024)(128)(4,1)} %bitcast.101), calls=%async_computation.1 | async-start | bytes 4194304
  196.7 6.9 %slice-start.1 = ((s8[6291456]{0:T(1024)(128)(4,1)}), s8[4194304]{0:T(1024)(128)(4,1)S(1)}, s32[]{:S(2)}) async-start(s8[6291456]{0:T(1024)(128)(4,1)} %bitcast.101), calls=%async_computation.2 | async-start | bytes 8388608
  200.7 2.8 copy-start.2
  201.9 1.6 copy-start.9
  205.6 1.8 copy-start.7
  207.4 0.9 copy-start.14
  208.3 1.4 copy-start.11
  210.2 14.0 %copy-start.19 = (bf16[768,768]{1,0:T(8,128)(2,1)S(1)}, bf16[768,768]{1,0:T(8,128)(2,1)}, u32[]{:S(2)}) copy-start(bf16[768,768]{1,0:T(8,128)(2,1)} %get-tuple-element.35) | copy-start | bytes 3538948
  224.2 2.8 copy-start.10
  227.3 1.1 copy-start.12
  271.1 16.4 %copy-start.3 = (f32[512,768]{1,0:T(8,128)S(1)}, f32[512,768]{1,0:T(8,128)}, u32[]{:S(2)}) copy-start(f32[512,768]{1,0:T(8,128)} %copy-done.2) | copy-start | bytes 4718596
  271.1 16.4 %copy-start.8 = (bf16[512,768]{1,0:T(8,128)(2,1)S(1)}, bf16[512,768]{1,0:T(8,128)(2,1)}, u32[]{:S(2)}) copy-start(bf16[512,768]{1,0:T(8,128)(2,1)} %get-tuple-element.44) | copy-start | bytes 2359300
  287.5 1.7 copy-start.17
  289.2 1.3 copy-start.16
Sparse Core Ops, SparseCore 0:
  151.8 44.8 all-reduce.5

commit v2 on v1

--- a/solution.py
+++ b/solution.py
@@ -112,26 +112,73 @@
     return mine, copies
 
 
+def pair_places(axis):
+    me = lax.axis_index(axis)
+    near = me + 1 - 2 * lax.rem(me, 2)
+    return me, near, lax.rem(me + 2, 4), lax.rem(near + 2, 4)
+
+
 def gather_steps(axes, sizes, src, out, sems):
     rows = src.shape[0]
-    mine, copies = spread(src, out, rows, axes, sizes, sems)
-    out[rows_at(mine, rows), :] = src[...]
-    yield
-    for copy in copies:
-        copy.wait_recv()
-    finish(copies)
-
-
-def scatter_steps(axes, sizes, src, out, landing, sems):
+    if sizes == (4,) and axes == ("clip",):
+        (axis,) = axes
+        me, near, far, _ = pair_places(axis)
+        mine = out.at[rows_at(me, rows)]
+        theirs = out.at[rows_at(far, rows)]
+        first = send(src, mine, sems, 0, {axis: far})
+        second = send(src, mine, sems, 1, {axis: near})
+        out[rows_at(me, rows), :] = src[...]
+        yield
+        first.wait_recv()
+        third = send(theirs, theirs, sems, 2, {axis: near})
+        yield
+        second.wait_recv()
+        third.wait_recv()
+        finish([first, second, third])
+    else:
+        mine, copies = spread(src, out, rows, axes, sizes, sems)
+        out[rows_at(mine, rows), :] = src[...]
+        yield
+        for copy in copies:
+            copy.wait_recv()
+        finish(copies)
+
+
+def chain_steps(axes, sizes, more_axes, more_sizes, src, out, held, sems, more_sems):
+    yield from gather_steps(axes, sizes, src, held, sems)
+    yield from gather_steps(more_axes, more_sizes, held, out, more_sems)
+
+
+def scatter_steps(axes, sizes, src, out, landing, part, sems):
     rows = out.shape[0]
-    mine, copies = deal(src, landing, rows, axes, sizes, sems)
-    yield
-    total = src[rows_at(mine, rows), :].astype(F32)
-    for slot, copy in enumerate(copies):
-        copy.wait_recv()
-        total = total + landing[slot].astype(F32)
-    out[...] = total.astype(out.dtype)
-    finish(copies)
+    if sizes == (4,) and axes == ("clip",):
+        (axis,) = axes
+        me, near, far, near_far = pair_places(axis)
+        copies = [
+            send(src.at[rows_at(near_far, rows)], landing.at[1], sems, 1, {axis: near}),
+            send(src.at[rows_at(near, rows)], landing.at[0], sems, 0, {axis: near}),
+        ]
+        yield
+        copies[0].wait_recv()
+        part[...] = (
+            src[rows_at(far, rows), :].astype(F32) + landing[1].astype(F32)
+        ).astype(part.dtype)
+        copies.append(send(part, landing.at[2], sems, 2, {axis: far}))
+        yield
+        copies[1].wait_recv()
+        copies[2].wait_recv()
+        total = src[rows_at(me, rows), :].astype(F32) + landing[0].astype(F32)
+        out[...] = (total + landing[2].astype(F32)).astype(out.dtype)
+        finish(copies)
+    else:
+        mine, copies = deal(src, landing, rows, axes, sizes, sems)
+        yield
+        total = src[rows_at(mine, rows), :].astype(F32)
+        for slot, copy in enumerate(copies):
+            copy.wait_recv()
+            total = total + landing[slot].astype(F32)
+        out[...] = total.astype(out.dtype)
+        finish(copies)
 
 
 def reduce_steps(axes, sizes, src, out, landing, sems, back_sems):
@@ -170,23 +217,11 @@
     finish(copies)
 
 
-def both_steps(axes, sizes, more_axes, more_sizes, src, out, landing, part, held, sems, more_sems):
-    rows = out.shape[0]
-    mine, copies = deal(src, landing, rows, axes, sizes, sems)
-    yield
-    total = src[rows_at(mine, rows), :].astype(F32)
-    for slot, copy in enumerate(copies):
-        copy.wait_recv()
-        total = total + landing[slot].astype(F32)
-    part[...] = total.astype(part.dtype)
-    at, mores = spread(part, held, rows, more_axes, more_sizes, more_sems)
-    held[rows_at(at, rows), :] = part[...]
-    yield
-    for copy in mores:
-        copy.wait_recv()
-    out[...] = sum_blocks(held, rows, len(mores) + 1).astype(out.dtype)
-    finish(copies)
-    finish(mores)
+def both_steps(
+    axes, sizes, more_axes, more_sizes, src, out, landing, part, owned, held, sems, more_sems
+):
+    yield from scatter_steps(axes, sizes, src, owned, landing, part, sems)
+    yield from share_steps(more_axes, more_sizes, owned, out, held, more_sems)
 
 
 def plan_of(kind, axes, sizes, more, array, out_type):
@@ -201,10 +236,25 @@
     if kind == "share":
         held = pltpu.VMEM((count * rows, cols), array.dtype)
         return (rows, cols), [held, pair], functools.partial(share_steps, axes, sizes)
+    if kind == "chain":
+        more_axes, more_sizes = more
+        more_count = 1
+        for size in more_sizes:
+            more_count *= size
+        return (
+            (more_count * count * rows, cols),
+            [
+                pltpu.VMEM((count * rows, cols), array.dtype),
+                pair,
+                pltpu.SemaphoreType.DMA((2, more_count - 1)),
+            ],
+            functools.partial(chain_steps, axes, sizes, more_axes, more_sizes),
+        )
     block = rows // count
+    one = pltpu.VMEM((block, cols), array.dtype)
     landing = pltpu.VMEM((peers, block, cols), array.dtype)
     if kind == "scatter":
-        return (block, cols), [landing, pair], functools.partial(scatter_steps, axes, sizes)
+        return (block, cols), [landing, one, pair], functools.partial(scatter_steps, axes, sizes)
     if kind == "reduce":
         return (
             (rows, cols),
@@ -219,7 +269,8 @@
         (block, cols),
         [
             landing,
-            pltpu.VMEM((block, cols), array.dtype),
+            one,
+            one,
             pltpu.VMEM((more_count * block, cols), array.dtype),
             pair,
             pltpu.SemaphoreType.DMA((2, more_count - 1)),
@@ -331,13 +382,14 @@
         jnp.stack([first_gain, first_shift, out_bias, second_gain, second_shift, reduce_bias]),
         ((0, 10), (0, wide - share)),
     )
-    attn_weights = jnp.concatenate([query_weight, key_weight, value_weight, out_weight.T], axis=1)
-    attn_full, vectors_full, frames_all = transfers(
+    attn_weights = jnp.concatenate([query_weight, key_weight, value_weight], axis=1)
+    qkv_full, vectors_full, out_blocks, frames_all = transfers(
         1,
         "gather_first",
         [
             ("gather", ("clip",), attn_weights, BF16),
             ("gather", ("clip",), vectors, BF16),
+            ("chain", ("tp",), out_weight, BF16, ("clip",)),
             ("gather", ("ctx",), frames, BF16),
         ],
     )
@@ -346,10 +398,11 @@
     gain_first, shift_first, out_shift, gain_second, shift_second, reduce_shift = [
         vectors_full[i] for i in range(6)
     ]
-    qkv_full = attn_full[:, : 3 * local_width]
-    kv_full = attn_full[:, local_width : 3 * local_width]
-    query_full = attn_full[:, :local_width]
-    out_full_t = attn_full[:, 3 * local_width :]
+    kv_full = qkv_full[:, local_width:]
+    query_full = qkv_full[:, :local_width]
+    out_blocks = out_blocks.reshape(clips, width, share)
+    out_all = out_blocks.transpose(1, 0, 2).reshape(width, width)
+    out_rows = lax.dynamic_slice_in_dim(out_all, lax.axis_index("tp") * local_width, local_width)
     inputs = frames.astype(F32)
     normed_one, factor_one = center_rows(inputs)
     first_norm = (normed_one * gain_first + shift_first).astype(BF16)
@@ -375,16 +428,19 @@
     mixed_full = run_acc / run_sum[..., None]
     log_total = run_max + jnp.log(run_sum)
     mixed_low = mixed_full.reshape(row_count, local_width).astype(BF16)
-    attn_sum, expand_full, reduce_full_t = transfers(
+    expand_full, reduce_full_t, mixed_all = transfers(
         2,
-        "attn_sum",
+        "gather_mixed",
         [
-            ("reduce", ("tp",), cols_inner(mixed_low, out_full_t).astype(BF16), BF16),
             ("gather", ("clip",), expand_weight, BF16),
             ("gather", ("clip",), reduce_weight.T, BF16),
+            ("gather", ("tp",), mixed_low, BF16),
         ],
     )
-    hidden = inputs + attn_sum.astype(F32) + out_shift
+    groups = width // local_width
+    mixed_all = mixed_all.reshape(groups, row_count, local_width)
+    mixed_all = mixed_all.transpose(1, 0, 2).reshape(row_count, width)
+    hidden = inputs + product(mixed_all, out_all) + out_shift
     normed_two, factor_two = center_rows(hidden)
     second_norm = (normed_two * gain_second + shift_second).astype(BF16)
     pre_act = product(second_norm, expand_full) + expand_bias.astype(F32)
@@ -399,24 +455,22 @@
     second_terms = cols_inner(grad_pre, expand_full).astype(BF16)
     grad_expand = rows_inner(second_norm, grad_pre).astype(BF16)
     grad_reduce_t = rows_inner(cotangent, act_low).astype(BF16)
-    grad_second, share_expand, share_reduce_t = transfers(
+    share_expand, share_reduce_t, grad_second = transfers(
         3,
         "grad_second",
         [
-            ("reduce", ("tp",), second_terms, BF16),
             ("scatter", ("clip",), grad_expand, BF16),
             ("scatter", ("clip",), grad_reduce_t, BF16),
+            ("reduce", ("tp",), second_terms, BF16),
         ],
     )
-    act_late, grad_second = lax.optimization_barrier((act_low, grad_second))
-    mlp_sum = lax.psum(cols_inner(act_late, reduce_full_t).astype(BF16), "tp").astype(F32)
-    layer_out = (hidden + mlp_sum + reduce_shift).astype(BF16)
+    mlp_terms = cols_inner(act_low, reduce_full_t).astype(BF16)
     grad_out = cotangent.astype(F32)
     grad_second = grad_second.astype(F32)
     grad_hidden = grad_out + norm_back(grad_second, normed_two, factor_two, gain_second)
     grad_attn = grad_hidden.astype(BF16)
     grad_out_weight_t = rows_inner(grad_attn, mixed_low).astype(BF16)
-    grad_mixed = product(grad_attn, out_full_t).astype(BF16)
+    grad_mixed = cols_inner(grad_attn, out_rows).astype(BF16)
     grad_heads = grad_mixed.reshape(row_count, head_count, DH)
     row_delta = jnp.sum(grad_heads.astype(F32) * mixed_full, axis=-1)
     weights_low, grad_scores = score_block(
@@ -432,7 +486,12 @@
         ],
         axis=1,
     ).astype(BF16)
-    (grad_kv_low,) = transfers(4, "grad_kv", [("scatter", ("ctx",), kv_terms, BF16)])
+    grad_kv_low, mlp_sum = transfers(
+        4,
+        "grad_kv",
+        [("scatter", ("ctx",), kv_terms, BF16), ("reduce", ("tp",), mlp_terms, BF16)],
+    )
+    layer_out = (hidden + mlp_sum.astype(F32) + reduce_shift).astype(BF16)
     grad_q_low = (grad_query * score_scale).reshape(row_count, local_width).astype(BF16)
     grad_qkv = jnp.concatenate([grad_q_low, grad_kv_low], axis=1)
     first_terms = cols_inner(grad_qkv, qkv_full).astype(BF16)
@@ -449,12 +508,12 @@
         qkv_bias[:local_width],
         qkv_bias[2 * local_width :],
     ]
-    grad_first, sum_attn, sum_expand, sum_reduce_t, early_sum = transfers(
+    sum_attn, grad_first, sum_expand, sum_reduce_t, early_sum = transfers(
         5,
         "grad_first",
         [
+            ("both", ("clip",), grad_attn_weights, F32, ("ctx",)),
             ("reduce", ("tp",), first_terms, BF16),
-            ("both", ("clip",), grad_attn_weights, F32, ("ctx",)),
             ("share", ("ctx",), share_expand, F32),
             ("share", ("ctx",), share_reduce_t, F32),
             ("share", ("clip", "ctx"), pack_vectors(early), F32),

time: 302 us -> 285 us (0.944)
  waiting for transfers between devices: 42.5 us -> 0 us
  Pallas kernels: 162 us -> 183 us
  local copies, waits for them, and re-layouts: 22.9 us -> 36.4 us
  between operations: 14.6 us -> 1.24 us
  matrix products: 31.3 us -> 41.2 us
    psum x1 -> x0, waiting for transfers between devices: 42.5 us -> none  [shards(): lax.psum(cols_inner(act_late, reduce_full_t).astype(BF16), 'tp').astype(F32)]
    pallas_call x6, Pallas kernels: 162 us -> 183 us  [transfers(): pl.pallas_call(kernel, name=name, out_shape=[jax.ShapeDtypeStruct(plan[0]...]
    reshape x0 -> x2, local copies, waits for them, and re-layouts: none -> 4.67 us  [the longest x1 2.48 us: shards(): out_blocks = out_blocks.reshape(clips, width, share)]
    reduce_sum x3 -> x2, other arithmetic: 4.69 us -> 1.58 us  [center_rows(): row_mean = jnp.mean(matrix, axis=-1, keepdims=True)]
    unnamed x62 -> x91, local copies, waits for them, and re-layouts: 6.03 us -> 7.27 us
  transfers between devices with their start and end apart: 1 -> 0, of which waited for: 1 -> 0; matrix products, arithmetic and copies ran while one was open for 1% -> 0% of each run, Pallas kernels for 0% -> 0%
where the time goes in v2:
time: 285 us; the launch traced here: 283 us
  Pallas kernels  183 us (64%)
  matrix products  41.2 us (14%)
  local copies, waits for them, and re-layouts  36.4 us (13%)
  other arithmetic  21.5 us (8%)
    pallas_call x6, Pallas kernels, transfers(): pl.pallas_call(kernel, name=name, out_shape=[jax.ShapeDtypeStruct(plan[0]...  183 us
    dot_general x5, matrix products, product(): return jnp.dot(left, right, preferred_element_type=jnp.float32)  10.2 us
    dot_general x4, matrix products, rows_inner(): lax.dot_general(left, right, (((0,), (0,)), ((), ())), preferred_element_...  8.27 us
    dot_general x4, matrix products, cols_inner(): lax.dot_general(left, right, (((1,), (1,)), ((), ())), preferred_element_...  7.93 us
    unnamed x91, local copies, waits for them, and re-layouts  7.27 us

profile of v2, /device:TPU:0, one launch (start us, length us, event | category | flops | bytes accessed | tf_op | source)
XLA Modules:
  0.0 283.0 jit_solution(6066307469205558320)
XLA Ops:
  0.7 0.7 stack.21
  1.4 0.7 stack.22
  2.1 0.7 convert_element_type.137
  2.7 0.7 stack.23
  3.4 0.7 stack.24
  4.1 0.7 stack.25
  4.7 0.7 stack.26
  5.4 0.7 pad_convert_fusion
  6.1 1.3 convert_reduce_fusion.3
  7.5 1.5 fusion.34
  9.6 0.8 pad_maximum_fusion.3.refs_0_
  10.4 28.8 %gather_first.1 = (bf16[768,576]{1,0:T(8,128)(2,1)}, bf16[64,256]{1,0:T(8,128)(2,1)}, bf16[3072,192]{1,0:T(8,128)(2,1)}, bf16[1024,768]{1,0:T(8,128)(2,1)}) custom-call(bf16[192,576]{1,0:T(8,128)(2,1)} %pad_maximum_fusion.3.refs_0_, bf16[16,256]{1,0:T(8,128)(2,1)} %pad.13.refs_1_, bf16[192,192]{1,0:T(8,128)(2,1)} %refs_2_.1, bf16[512,768]{1,0:T(8,128)(2,1)} %refs_3_.1), custom_call_target="tpu_custom_call" | custom-call | tf_op jit(solution)/shard_map/gather_first/pallas_call | solution.py:320
  39.2 0.8 convert_bitcast_fusion
  40.1 0.7 add.163
  40.8 2.5 copy.63
  44.9 1.3 add_convert_fusion.2
  46.3 1.2 copy-done.1
  48.1 1.0 bitcast_reduce_fusion
  49.2 1.0 fusion.5
  50.2 1.6 copy-done
  51.8 1.9 fusion.94
  53.7 0.8 copy.61.refs_2_
  54.5 24.8 %gather_mixed.1 = (bf16[768,768]{1,0:T(8,128)(2,1)}, bf16[768,768]{1,0:T(8,128)(2,1)}, bf16[2048,192]{1,0:T(8,128)(2,1)}) custom-call(bf16[192,768]{1,0:T(8,128)(2,1)} %refs_0_.1, bf16[192,768]{1,0:T(8,128)(2,1)} %bitcast.130, bf16[512,192]{1,0:T(8,128)(2,1)} %copy.61.refs_2_), custom_call_target="tpu_custom_call" | custom-call | tf_op jit(solution)/shard_map/gather_mixed/pallas_call | solution.py:320
  79.3 2.2 copy.62
  81.5 2.4 fusion.95
  84.3 0.9 copy-done.40
  85.2 4.0 %multiply_convert_fusion = (bf16[512,768]{1,0:T(8,128)(2,1)S(1)}, f32[512,768]{1,0:T(8,128)S(1)}, f32[512,768]{1,0:T(8,128)S(1)}) fusion(f32[768]{0:T(1024)S(1)} %convert_element_type.144, bf16[768,768]{1,0:T(8,128)(2,1)S(1)} %copy-done.40, f32[512,768]{1,0:T(8,128)S(1)} %get-tuple-element.143, f32[768]{0:T(1024)S(1)} %add.155, f32[768]{0:T(1024)S(1)} %mul.194, ...), kind=kOutput, calls=%fused_computation.72 | convolution fusion | flops 631898112 | bytes 6697984 | tf_op jit(solution)/shard_map/dot_general | solution.py:29
  89.3 1.8 convert_reduce_fusion.5
  91.1 1.8 convolution_convert_fusion.3.refs_1_
  92.9 1.7 convolution_convert_fusion.4.refs_2_
  94.5 1.9 fusion.61.refs_1_
  96.4 2.1 convolution_convert_fusion.1.refs_0_
  98.5 41.8 %grad_second.1 = (bf16[192,768]{1,0:T(8,128)(2,1)}, bf16[192,768]{1,0:T(8,128)(2,1)}, bf16[512,768]{1,0:T(8,128)(2,1)}) custom-call(bf16[768,768]{1,0:T(8,128)(2,1)} %convolution_convert_fusion.1.refs_0_, bf16[768,768]{1,0:T(8,128)(2,1)} %fusion.61.refs_1_, bf16[512,768]{1,0:T(8,128)(2,1)} %convolution_convert_fusion.4.refs_2_), custom_call_target="tpu_custom_call" | custom-call | tf_op jit(solution)/shard_map/grad_second/pallas_call | solution.py:320
  140.4 2.6 fusion.41
  142.9 1.3 convert_reduce_fusion.6
  144.3 1.7 convolution_convert_fusion.7
  146.0 0.7 copy-done.8
  146.6 0.7 multiply_reduce_fusion.1
  147.3 1.0 convolution_convert_fusion.6
  148.4 2.1 copy.72
  150.5 4.9 %fusion.65 = bf16[3,64,1024]{2,1,0:T(8,128)(2,1)} fusion(bf16[512,3,64]{0,2,1:T(8,128)(2,1)} %bitcast.115, f32[3,1024,512]{2,1,0:T(8,128)} %copy-done, f32[512,3]{0,1:T(4,128)S(1)} %log_add_fusion), kind=kOutput, calls=%fused_computation.105 | convolution fusion | flops 206241792 | bytes 6887424 | tf_op jit(solution)/shard_map/qhk,qhd->khd/dot_general | solution.py:481
  155.4 4.6 %fusion.1 = bf16[512,3,1024]{0,2,1:T(8,128)(2,1)S(1)} fusion(f32[3,1024,512]{2,1,0:T(8,128)} %copy-done, f32[512,3]{0,1:T(4,128)S(1)} %copy-done.25, f32[512,3]{0,1:T(4,128)S(1)} %log_add_fusion, bf16[1024,3,64]{0,2,1:T(8,128)(2,1)S(1)} %bitcast.111, bf16[512,3,64]{0,2,1:T(8,128)(2,1)S(1)} %bitcast.116), kind=kOutput, calls=%fused_computation.2 | convolution fusion | flops 209190912 | bytes 10039296 | tf_op jit(solution)/shard_map/qhd,khd->qhk/dot_general | solution.py:50
  160.0 1.3 fusion.71
  161.3 1.1 fusion.64
  162.4 1.8 copy.70
  164.2 2.0 copy.68
  166.2 1.0 copy.67
  167.2 2.5 pad_maximum_fusion.1.refs_0_
  169.6 38.9 %grad_kv.1 = (bf16[512,384]{1,0:T(8,128)(2,1)}, bf16[512,768]{1,0:T(8,128)(2,1)}) custom-call(bf16[1024,384]{1,0:T(8,128)(2,1)} %pad_maximum_fusion.1.refs_0_, bf16[512,768]{1,0:T(8,128)(2,1)} %convolution_convert_fusion.3.refs_1_), custom_call_target="tpu_custom_call" | custom-call | tf_op jit(solution)/shard_map/grad_kv/pallas_call | solution.py:320
  208.6 2.8 convolution_convert_fusion.5.refs_1_
  211.4 1.1 add_convert_fusion
  213.6 3.3 %convolution_convert_fusion.2 = bf16[768,576]{0,1:T(8,128)(2,1)} fusion(bf16[512,384]{1,0:T(8,128)(2,1)} %get-tuple-element.43, bf16[512,192]{1,0:T(8,128)(2,1)S(1)} %copy-done.14, bf16[512,768]{1,0:T(8,128)(2,1)} %refs_3_.1, f32[768]{0:T(1024)S(1)} %copy-done.37, f32[768]{0:T(1024)S(1)} %mul.181, f32[512]{0:T(512)S(1)} %copy-done.30, f32[512]{0:T(512)S(1)} %copy-done.27), kind=kOutput, calls=%fused_computation.97 | convolution fusion | flops 456966144 | bytes 2271232 | tf_op jit(solution)/shard_map/dot_general | solution.py:33
  216.8 1.6 copy.71
  218.4 1.2 pad_maximum_fusion.refs_0_
  219.6 42.4 %grad_first.1 = (f32[192,768]{1,0:T(8,128)}, bf16[512,768]{1,0:T(8,128)(2,1)}, f32[192,768]{1,0:T(8,128)}, f32[192,768]{1,0:T(8,128)}, f32[8,640]{1,0:T(8,128)}) custom-call(bf16[768,768]{1,0:T(8,128)(2,1)} %pad_maximum_fusion.refs_0_, bf16[512,768]{1,0:T(8,128)(2,1)} %convolution_convert_fusion.5.refs_1_, bf16[192,768]{1,0:T(8,128)(2,1)} %get-tuple-element.44.refs_2_, ...), custom_call_target="tpu_custom_call" | custom-call | tf_op jit(solution)/shard_map/grad_first/pallas_call | solution.py:320
  262.1 2.0 fusion.42
  264.7 6.1 %gain_sums.1 = f32[8,256]{1,0:T(8,128)} custom-call(f32[8,256]{1,0:T(8,128)} %reshape.175.refs_0_), custom_call_target="tpu_custom_call" | custom-call | tf_op jit(solution)/shard_map/gain_sums/pallas_call | solution.py:320
  270.8 0.8 fusion.92
  272.2 1.7 fusion.33
  274.6 0.6 fusion.91
  278.4 2.2 slice_bitcast_fusion
  280.6 0.8 copy.73
  281.3 0.8 copy.81
  282.2 0.8 copy.82
  (125 shorter events, 9.5 us)
Async XLA Ops:
  0.7 8.9 %copy-start.39 = (bf16[768]{0:T(1024)(128)(2,1)S(1)}, bf16[768]{0:T(1024)(128)(2,1)}, u32[]{:S(2)}) copy-start(bf16[768]{0:T(1024)(128)(2,1)} %param.31) | copy-start | bytes 4612
  0.7 8.9 %copy-start.22 = (bf16[192,192]{1,0:T(8,128)(2,1)S(1)}, bf16[192,192]{1,0:T(8,128)(2,1)}, u32[]{:S(2)}) copy-start(bf16[192,192]{1,0:T(8,128)(2,1)} %param.24) | copy-start | bytes 221188
  0.7 8.9 %copy-start.23 = (bf16[192,192]{1,0:T(8,128)(2,1)S(1)}, bf16[192,192]{1,0:T(8,128)(2,1)}, u32[]{:S(2)}) copy-start(bf16[192,192]{1,0:T(8,128)(2,1)} %param.23) | copy-start | bytes 221188
  0.7 8.9 %copy-start.24 = (bf16[192,192]{1,0:T(8,128)(2,1)S(1)}, bf16[192,192]{1,0:T(8,128)(2,1)}, u32[]{:S(2)}) copy-start(bf16[192,192]{1,0:T(8,128)(2,1)} %param.21) | copy-start | bytes 221188
  7.4 38.8 %copy-start.26 = (f32[512]{0:T(512)}, f32[512]{0:T(512)S(1)}, u32[]{:S(2)}) copy-start(f32[512]{0:T(512)S(1)} %broadcast_multiply_fusion.6) | copy-start | bytes 6148
  9.0 37.3 %copy-start.29 = (f32[512]{0:T(512)}, f32[512]{0:T(512)S(1)}, u32[]{:S(2)}) copy-start(f32[512]{0:T(512)S(1)} %add_rsqrt_fusion.2) | copy-start | bytes 6148
  39.2 4.5 %copy-start.3 = (bf16[1024,768]{1,0:T(8,128)(2,1)S(1)}, bf16[1024,768]{1,0:T(8,128)(2,1)}, u32[]{:S(2)}) copy-start(bf16[1024,768]{1,0:T(8,128)(2,1)} %get-tuple-element.34) | copy-start | bytes 4718596
  43.5 2.8 copy-start.36
  43.6 1.2 copy-start.42
  46.2 1.3 copy-start.1
  46.3 2.9 %copy-start.4 = (bf16[1024,192]{0,1:T(8,128)(2,1)}, bf16[1024,192]{0,1:T(8,128)(2,1)S(1)}, u32[]{:S(2)}) copy-start(bf16[1024,192]{0,1:T(8,128)(2,1)S(1)} %get-tuple-element.121) | copy-start | bytes 1179652
  48.1 1.1 copy-start.15
  49.2 2.7 copy-start
  53.7 27.8 %copy-start.10 = (bf16[512,3,64]{0,2,1:T(8,128)(2,1)}, bf16[512,3,64]{0,2,1:T(8,128)(2,1)S(1)}, u32[]{:S(2)}) copy-start(bf16[512,3,64]{0,2,1:T(8,128)(2,1)S(1)} %get-tuple-element.140) | copy-start | bytes 589828
  83.9 1.3 copy-start.40
  85.2 4.1 %copy-start.18 = (bf16[512,768]{1,0:T(8,128)(2,1)S(1)}, bf16[512,768]{1,0:T(8,128)(2,1)}, u32[]{:S(2)}) copy-start(bf16[512,768]{1,0:T(8,128)(2,1)} %param.18) | copy-start | bytes 2359300
  85.2 4.1 %copy-start.41 = (bf16[768,768]{1,0:T(8,128)(2,1)S(1)}, bf16[768,768]{1,0:T(8,128)(2,1)}, u32[]{:S(2)}) copy-start(bf16[768,768]{1,0:T(8,128)(2,1)} %get-tuple-element.40) | copy-start | bytes 3538948
  140.4 2.6 copy-start.7
  144.3 2.4 copy-start.12
  144.3 3.0 %copy-start.11 = (bf16[512,3,64]{0,2,1:T(8,128)(2,1)S(1)}, bf16[512,3,64]{0,2,1:T(8,128)(2,1)}, u32[]{:S(2)}) copy-start(bf16[512,3,64]{0,2,1:T(8,128)(2,1)} %copy-done.10) | copy-start | bytes 589828
  146.0 0.7 copy-start.8
  150.5 4.9 %copy-start.9 = (bf16[512,192]{0,1:T(8,128)(2,1)S(1)}, bf16[512,192]{0,1:T(8,128)(2,1)}, u32[]{:S(2)}) copy-start(bf16[512,192]{0,1:T(8,128)(2,1)} %copy-done.8) | copy-start | bytes 589828
  150.5 4.9 %copy-start.25 = (f32[512,3]{0,1:T(4,128)S(1)}, f32[512,3]{0,1:T(4,128)}, u32[]{:S(2)}) copy-start(f32[512,3]{0,1:T(4,128)} %multiply_reduce_fusion.1) | copy-start | bytes 18436
  155.4 4.6 %copy-start.5 = (bf16[1024,192]{0,1:T(8,128)(2,1)S(1)}, bf16[1024,192]{0,1:T(8,128)(2,1)}, u32[]{:S(2)}) copy-start(bf16[1024,192]{0,1:T(8,128)(2,1)} %copy-done.4) | copy-start | bytes 1179652
  160.0 1.3 copy-start.16
  167.2 41.4 %copy-start.14 = (bf16[512,192]{1,0:T(8,128)(2,1)S(1)}, bf16[512,192]{1,0:T(8,128)(2,1)}, u32[]{:S(2)}) copy-start(bf16[512,192]{1,0:T(8,128)(2,1)} %copy.70) | copy-start | bytes 589828
  167.2 41.4 %copy-start.43 = (bf16[768,576]{1,0:T(8,128)(2,1)S(1)}, bf16[768,576]{1,0:T(8,128)(2,1)}, u32[]{:S(2)}) copy-start(bf16[768,576]{1,0:T(8,128)(2,1)} %get-tuple-element.36) | copy-start | bytes 2654212
  208.5 2.8 copy-start.17
  208.5 2.8 copy-start.31
  211.3 1.2 copy-start.21
  211.3 1.5 copy-start.32
  211.3 1.5 copy-start.33
  211.3 1.5 copy-start.34
  211.4 1.5 copy-start.35
  211.4 1.5 copy-start.38
  211.4 2.2 copy-start.27
  211.4 2.2 copy-start.30
  211.4 2.2 copy-start.37
  216.8 1.6 copy-start.13
  219.6 42.4 %copy-start.2 = (bf16[512,768]{1,0:T(8,128)(2,1)S(1)}, bf16[512,768]{1,0:T(8,128)(2,1)}, u32[]{:S(2)}) copy-start(bf16[512,768]{1,0:T(8,128)(2,1)} %refs_3_.1) | copy-start | bytes 2359300
  262.0 10.2 %copy-start.6 = (bf16[512,768]{1,0:T(8,128)(2,1)S(1)}, bf16[512,768]{1,0:T(8,128)(2,1)}, u32[]{:S(2)}) copy-start(bf16[512,768]{1,0:T(8,128)(2,1)} %get-tuple-element.46) | copy-start | bytes 2359300
  272.2 2.4 copy-start.28
  273.9 7.4 %copy-start.20 = (f32[192,768]{1,0:T(8,128)S(1)}, f32[192,768]{1,0:T(8,128)}, u32[]{:S(2)}) copy-start(f32[192,768]{1,0:T(8,128)} %get-tuple-element.179) | copy-start | bytes 1769476
  278.4 3.8 %copy-start.19 = (f32[192,768]{1,0:T(8,128)S(1)}, f32[192,768]{1,0:T(8,128)}, u32[]{:S(2)}) copy-start(f32[192,768]{1,0:T(8,128)} %get-tuple-element.50) | copy-start | bytes 1769476

commit v3 on v2

--- a/solution.py
+++ b/solution.py
@@ -377,11 +377,13 @@
     hidden_width = expand_weight.shape[1]
     clips = lax.axis_size("clip")
     clip_at = lax.axis_index("clip") * share
-    wide = -(-share // 128) * 128
-    vectors = jnp.pad(
-        jnp.stack([first_gain, first_shift, out_bias, second_gain, second_shift, reduce_bias]),
-        ((0, 10), (0, wide - share)),
-    )
+    flat = jnp.concatenate(
+        [first_gain, first_shift, out_bias, second_gain, second_shift, reduce_bias]
+    )
+    wide = -(-flat.shape[0] // (16 * 128)) * 128
+    vectors = jnp.pad(flat, (0, 16 * wide - flat.shape[0])).reshape(16, wide)
+    half = local_width // 2
+    out_packed = jnp.concatenate([out_weight[:half], out_weight[half:]], axis=1)
     attn_weights = jnp.concatenate([query_weight, key_weight, value_weight], axis=1)
     qkv_full, vectors_full, out_blocks, frames_all = transfers(
         1,
@@ -389,19 +391,20 @@
         [
             ("gather", ("clip",), attn_weights, BF16),
             ("gather", ("clip",), vectors, BF16),
-            ("chain", ("tp",), out_weight, BF16, ("clip",)),
+            ("chain", ("tp",), out_packed, BF16, ("clip",)),
             ("gather", ("ctx",), frames, BF16),
         ],
     )
-    vectors_full = vectors_full.reshape(clips, 16, wide)[:, :6, :share]
+    vectors_full = vectors_full.reshape(clips, 16 * wide)[:, : 6 * share].reshape(clips, 6, share)
     vectors_full = vectors_full.transpose(1, 0, 2).reshape(6, width).astype(F32)
     gain_first, shift_first, out_shift, gain_second, shift_second, reduce_shift = [
         vectors_full[i] for i in range(6)
     ]
     kv_full = qkv_full[:, local_width:]
     query_full = qkv_full[:, :local_width]
-    out_blocks = out_blocks.reshape(clips, width, share)
-    out_all = out_blocks.transpose(1, 0, 2).reshape(width, width)
+    groups = width // local_width
+    out_blocks = out_blocks.reshape(clips, groups, half, 2, share)
+    out_all = out_blocks.transpose(1, 3, 2, 0, 4).reshape(width, width)
     out_rows = lax.dynamic_slice_in_dim(out_all, lax.axis_index("tp") * local_width, local_width)
     inputs = frames.astype(F32)
     normed_one, factor_one = center_rows(inputs)
@@ -434,13 +437,10 @@
         [
             ("gather", ("clip",), expand_weight, BF16),
             ("gather", ("clip",), reduce_weight.T, BF16),
-            ("gather", ("tp",), mixed_low, BF16),
-        ],
-    )
-    groups = width // local_width
-    mixed_all = mixed_all.reshape(groups, row_count, local_width)
-    mixed_all = mixed_all.transpose(1, 0, 2).reshape(row_count, width)
-    hidden = inputs + product(mixed_all, out_all) + out_shift
+            ("gather", ("tp",), mixed_low.T, BF16),
+        ],
+    )
+    hidden = inputs + rows_inner(mixed_all, out_all) + out_shift
     normed_two, factor_two = center_rows(hidden)
     second_norm = (normed_two * gain_second + shift_second).astype(BF16)
     pre_act = product(second_norm, expand_full) + expand_bias.astype(F32)
@@ -464,7 +464,19 @@
             ("reduce", ("tp",), second_terms, BF16),
         ],
     )
-    mlp_terms = cols_inner(act_low, reduce_full_t).astype(BF16)
+    act_late, grad_second = lax.optimization_barrier((act_low, grad_second))
+    mlp_terms = cols_inner(act_late, reduce_full_t).astype(BF16)
+    tp_size = lax.axis_size("tp")
+    tp_at = lax.axis_index("tp")
+    part_rows = row_count // tp_size
+
+    def mlp_block(index):
+        return lax.dynamic_slice_in_dim(mlp_terms, index * part_rows, part_rows)
+
+    mlp_parts = [mlp_block(tp_at)]
+    for step in range(1, tp_size):
+        ring = [(i, (i + step) % tp_size) for i in range(tp_size)]
+        mlp_parts.append(lax.ppermute(mlp_block((tp_at + step) % tp_size), "tp", ring))
     grad_out = cotangent.astype(F32)
     grad_second = grad_second.astype(F32)
     grad_hidden = grad_out + norm_back(grad_second, normed_two, factor_two, gain_second)
@@ -486,10 +498,16 @@
         ],
         axis=1,
     ).astype(BF16)
+    mlp_part = mlp_parts[0].astype(F32)
+    for part in mlp_parts[1:]:
+        mlp_part = mlp_part + part.astype(F32)
     grad_kv_low, mlp_sum = transfers(
         4,
         "grad_kv",
-        [("scatter", ("ctx",), kv_terms, BF16), ("reduce", ("tp",), mlp_terms, BF16)],
+        [
+            ("scatter", ("ctx",), kv_terms, BF16),
+            ("gather", ("tp",), mlp_part.astype(BF16), BF16),
+        ],
     )
     layer_out = (hidden + mlp_sum.astype(F32) + reduce_shift).astype(BF16)
     grad_q_low = (grad_query * score_scale).reshape(row_count, local_width).astype(BF16)
@@ -526,31 +544,28 @@
     )
     frames_grad = grad_hidden + norm_back(grad_first, normed_one, factor_one, gain_first)
 
-    def mine(vector):
-        return lax.dynamic_slice(vector, (clip_at,), (share,))
-
-    sums = unpack_vectors(
-        early_sum, [width] * 4 + [hidden_width, local_width, local_width]
-    )
-    gain_one, shift_one = unpack_vectors(late_sum, [width] * 2)
+    sums = unpack_vectors(early_sum, [4 * width, hidden_width, local_width, local_width])
+    (late_sums,) = unpack_vectors(late_sum, [2 * width])
+    shared = jnp.concatenate([sums[0], late_sums]).reshape(6, width)
+    shared = lax.dynamic_slice(shared, (0, clip_at), (6, share))
     return (
         layer_out,
         frames_grad,
-        mine(gain_one),
-        mine(shift_one),
+        shared[4],
+        shared[5],
         sum_attn[:, :local_width],
-        sums[5],
+        sums[2],
         sum_attn[:, local_width : 2 * local_width],
         sum_attn[:, 2 * local_width : 3 * local_width],
-        sums[6],
+        sums[3],
         sum_attn[:, 3 * local_width :].T,
-        mine(sums[3]),
-        mine(sums[1]),
-        mine(sums[2]),
+        shared[3],
+        shared[1],
+        shared[2],
         sum_expand,
-        sums[4],
+        sums[1],
         sum_reduce_t.T,
-        mine(sums[0]),
+        shared[0],
     )
 
 

time: 285 us -> 257 us (0.902)
  Pallas kernels: 183 us -> 156 us
  local copies, waits for them, and re-layouts: 36.4 us -> 26.8 us
  starting transfers between devices: 0 us -> 6.8 us
  matrix products: 41.2 us -> 35.4 us
  other arithmetic: 21.5 us -> 25.6 us
    pallas_call x6, Pallas kernels: 183 us -> 156 us  [transfers(): pl.pallas_call(kernel, name=name, out_shape=[jax.ShapeDtypeStruct(plan[0]...]
    ppermute x0 -> x3, starting transfers between devices: none -> 6.8 us  [shards(): lax.ppermute(mlp_block((tp_at + step) % tp_size), 'tp', ring)]
    reshape x2 -> x6, local copies, waits for them, and re-layouts: 4.67 us -> 11.3 us  [the longest x2 6.44 us: shards(): out_blocks = out_blocks.reshape(clips, groups, half, 2, share)]
    another operation x7 -> x0, local copies, waits for them, and re-layouts: 4.03 us -> none  [shards(): jnp.stack([first_gain, first_shift, out_bias, second_gain, second_shift,...]
    dynamic_slice x6 -> x1, local copies, waits for them, and re-layouts: 3.81 us -> 0.92 us  [mlp_block(): return lax.dynamic_slice_in_dim(mlp_terms, index * part_rows, part_rows)]
    dot_general x5 -> x4, matrix products: 10.2 us -> 8.44 us  [product(): return jnp.dot(left, right, preferred_element_type=jnp.float32)]
    unnamed x91 -> x77, local copies, waits for them, and re-layouts: 7.27 us -> 5.95 us
    dot_general x4 -> x5, matrix products: 8.27 us -> 8.63 us  [rows_inner(): lax.dot_general(left, right, (((0,), (0,)), ((), ())), preferred_element_...]
  transfers between devices with their start and end apart: 0 -> 3, of which waited for: 0 -> 0; matrix products, arithmetic and copies ran while one was open for 0% -> 7% of each run, Pallas kernels for 0% -> 0%
where the time goes in v3:
time: 257 us; the launch traced here: 252 us
  Pallas kernels  156 us (61%)
  matrix products  35.4 us (14%)
  local copies, waits for them, and re-layouts  26.8 us (10%)
  other arithmetic  25.6 us (10%)
  starting transfers between devices  6.8 us (3%)
    pallas_call x6, Pallas kernels, transfers(): pl.pallas_call(kernel, name=name, out_shape=[jax.ShapeDtypeStruct(plan[0]...  156 us
    dot_general x5, matrix products, rows_inner(): lax.dot_general(left, right, (((0,), (0,)), ((), ())), preferred_element_...  8.63 us
    dot_general x4, matrix products, product(): return jnp.dot(left, right, preferred_element_type=jnp.float32)  8.44 us
    dot_general x4, matrix products, cols_inner(): lax.dot_general(left, right, (((1,), (1,)), ((), ())), preferred_element_...  7.03 us
    ppermute x3, starting transfers between devices, shards(): lax.ppermute(mlp_block((tp_at + step) % tp_size), 'tp', ring)  6.8 us
    reshape x2, local copies, waits for them, and re-layouts, shards(): out_blocks = out_blocks.reshape(clips, groups, half, 2, share)  6.44 us
    unnamed x77, local copies, waits for them, and re-layouts  5.95 us
  transfers between devices with their start and end apart: 3, of which 0 were waited for; matrix products, arithmetic and copies ran while one was open for 7% of the time, Pallas kernels for 0%

profile of v3, /device:TPU:0, one launch (start us, length us, event | category | flops | bytes accessed | tf_op | source)
XLA Modules:
  0.0 252.2 jit_solution(10122491261224553669)
XLA Ops:
  0.8 0.8 convert_element_type.157
  1.6 0.7 pad_convert_fusion
  2.3 1.3 convert_reduce_fusion.3
  3.7 1.5 fusion.34
  5.3 0.6 pad_bitcast_fusion.refs_1_
  5.9 0.7 pad_maximum_fusion.6.refs_2_
  6.7 0.8 pad_maximum_fusion.3.refs_0_
  7.5 28.5 %gather_first.1 = (bf16[768,576]{1,0:T(8,128)(2,1)}, bf16[64,128]{1,0:T(8,128)(2,1)}, bf16[1536,384]{1,0:T(8,128)(2,1)}, bf16[1024,768]{1,0:T(8,128)(2,1)}) custom-call(bf16[192,576]{1,0:T(8,128)(2,1)} %pad_maximum_fusion.3.refs_0_, bf16[16,128]{1,0:T(8,128)(2,1)} %pad_bitcast_fusion.refs_1_, bf16[96,384]{1,0:T(8,128)(2,1)} %pad_maximum_fusion.6.refs_2_, ...), custom_call_target="tpu_custom_call" | custom-call | tf_op jit(solution)/shard_map/gather_first/pallas_call | solution.py:320
  36.0 0.8 reshape.166
  36.8 1.8 convert_reduce_fusion
  38.6 0.6 fusion.9
  39.6 1.3 add_convert_fusion.2
  41.2 4.1 %reshape.170 = bf16[4,4,96,2,192]{4,3,2,1,0:T(2,128)(2,1)S(1)} reshape(bf16[1536,384]{1,0:T(8,128)(2,1)} %get-tuple-element.40) | data formatting | bytes 2359296 | tf_op jit(solution)/shard_map/reshape | solution.py:406
  45.3 2.4 copy.75
  47.6 3.4 %reshape.171 = bf16[768,768]{1,0:T(8,128)(2,1)S(1)} reshape(bf16[4,2,96,4,192]{4,3,2,1,0:T(4,128)(2,1)} %bitcast.116) | data formatting | bytes 2359296 | tf_op jit(solution)/shard_map/reshape | solution.py:407
  51.1 1.9 fusion.72
  53.0 1.0 bitcast_reduce_fusion
  54.1 1.0 fusion.5
  55.1 1.6 copy-done
  56.7 1.9 fusion.93
  58.7 20.4 %gather_mixed.1 = (bf16[768,768]{1,0:T(8,128)(2,1)}, bf16[768,768]{1,0:T(8,128)(2,1)}, bf16[768,512]{1,0:T(8,128)(2,1)}) custom-call(bf16[192,768]{1,0:T(8,128)(2,1)} %refs_0_.1, bf16[192,768]{1,0:T(8,128)(2,1)} %bitcast.132, bf16[192,512]{1,0:T(8,128)(2,1)} %bitcast.124), custom_call_target="tpu_custom_call" | custom-call | tf_op jit(solution)/shard_map/gather_mixed/pallas_call | solution.py:320
  79.1 2.1 fusion.94
  81.5 1.5 copy-done.32
  83.0 4.0 %multiply_convert_fusion = (bf16[512,768]{1,0:T(8,128)(2,1)S(1)}, f32[512,768]{1,0:T(8,128)S(1)}, f32[512,768]{1,0:T(8,128)S(1)}) fusion(f32[768]{0:T(1024)S(1)} %convert_element_type.164, bf16[768,768]{1,0:T(8,128)(2,1)S(1)} %copy-done.32, f32[512,768]{1,0:T(8,128)S(1)} %get-tuple-element.151, f32[768]{0:T(1024)S(1)} %add.190, f32[768]{0:T(1024)S(1)} %mul.206, ...), kind=kOutput, calls=%fused_computation.73 | convolution fusion | flops 631898112 | bytes 6697984 | tf_op jit(solution)/shard_map/dot_general | solution.py:29
  87.1 1.2 convert_reduce_fusion.5
  88.2 1.7 convolution_convert_fusion.4.refs_2_
  89.9 2.1 convolution_convert_fusion.1.refs_0_
  92.0 2.1 fusion.61.refs_1_
  94.1 42.1 %grad_second.1 = (bf16[192,768]{1,0:T(8,128)(2,1)}, bf16[192,768]{1,0:T(8,128)(2,1)}, bf16[512,768]{1,0:T(8,128)(2,1)}) custom-call(bf16[768,768]{1,0:T(8,128)(2,1)} %convolution_convert_fusion.1.refs_0_, bf16[768,768]{1,0:T(8,128)(2,1)} %fusion.61.refs_1_, bf16[512,768]{1,0:T(8,128)(2,1)} %convolution_convert_fusion.4.refs_2_), custom_call_target="tpu_custom_call" | custom-call | tf_op jit(solution)/shard_map/grad_second/pallas_call | solution.py:320
  136.3 0.8 convolution_convert_fusion.3
  137.1 0.9 constant_dynamic-slice_fusion.3
  138.0 2.7 %collective-permute-start = (bf16[128,768]{1,0:T(8,128)(2,1)}, bf16[128,768]{1,0:T(8,128)(2,1)}, u32[]{:S(2)}, u32[]{:S(2)}) collective-permute-start(bf16[128,768]{1,0:T(8,128)(2,1)} %get-tuple-element.125), channel_id=1, source_target_pairs={{0,1},{1,2},{2,3},{3,0},{4,5},{5,6},{6,7},{7,4},{8,9},{9,10},{10,1... | collective-permute-start | bytes 589832 | tf_op jit(solution)/shard_map/ppermute | solution.py:479
  140.7 1.2 collective-permute-start.2
  141.8 3.0 %collective-permute-start.1 = (bf16[128,768]{1,0:T(8,128)(2,1)}, bf16[128,768]{1,0:T(8,128)(2,1)}, u32[]{:S(2)}, u32[]{:S(2)}) collective-permute-start(bf16[128,768]{1,0:T(8,128)(2,1)} %get-tuple-element.127), channel_id=1, source_target_pairs={{0,2},{1,3},{2,0},{3,1},{4,6},{5,7},{6,4},{7,5},{8,10},{9,11},{10,... | collective-permute-start | bytes 589832 | tf_op jit(solution)/shard_map/ppermute | solution.py:479
  144.9 2.5 %fusion.41 = (f32[768]{0:T(1024)S(1)}, f32[512]{0:T(512)S(1)}, f32[512]{0:T(512)S(1)}, f32[768]{0:T(1024)S(1)}) fusion(bf16[512,768]{1,0:T(8,128)(2,1)} %get-tuple-element.44, f32[512,768]{1,0:T(8,128)} %copy-done.1, f32[512]{0:T(512)S(1)} %add_rsqrt_fusion.1, f32[512]{0:T(512)S(1)} %broadcast_multiply_fusion.5, f32[768]{0:T(1024)S(1)} %mul.206), kind=kLoop, calls=%fused_computation.57 | loop fusion | flops 3929600 | bytes 2376704 | tf_op jit(solution)/shard_map/reduce_sum | solution.py:522
  147.4 2.6 %convert_reduce_fusion.6 = (f32[768]{0:T(1024)S(1)}, f32[512,768]{1,0:T(8,128)S(1)}, f32[768]{0:T(1024)S(1)}) fusion(f32[512]{0:T(512)S(1)} %get-tuple-element.155, f32[512,768]{1,0:T(8,128)} %copy-done.1, f32[512]{0:T(512)S(1)} %broadcast_multiply_fusion.5, f32[512]{0:T(512)S(1)} %get-tuple-element.156, f32[768]{0:T(1024)S(1)} %mul.206, ...), kind=kLoop, calls=%fused_computation.71 | loop fusion | flops 5503488 | bytes 4736000 | tf_op jit(solution)/shard_map/reduce_sum | solution.py:524
  150.0 1.8 convolution_convert_fusion.7
  151.9 4.9 %fusion.65 = bf16[3,64,1024]{2,1,0:T(8,128)(2,1)} fusion(bf16[512,3,64]{0,2,1:T(8,128)(2,1)S(1)} %bitcast.122, f32[3,1024,512]{2,1,0:T(8,128)} %copy-done, f32[512,3]{0,1:T(4,128)S(1)} %log_add_fusion), kind=kOutput, calls=%fused_computation.106 | convolution fusion | flops 206241792 | bytes 6887424 | tf_op jit(solution)/shard_map/qhk,qhd->khd/dot_general | solution.py:493
  156.8 1.8 fusion.1
  158.6 0.6 fusion.71
  159.2 1.1 fusion.64
  161.7 1.2 pad_maximum_fusion.1.refs_0_
  162.9 2.0 add_convert_fusion.3.refs_1_
  164.9 15.8 %grad_kv.1 = (bf16[512,384]{1,0:T(8,128)(2,1)}, bf16[512,768]{1,0:T(8,128)(2,1)}) custom-call(bf16[1024,384]{1,0:T(8,128)(2,1)} %pad_maximum_fusion.1.refs_0_, bf16[128,768]{1,0:T(8,128)(2,1)} %add_convert_fusion.3.refs_1_), custom_call_target="tpu_custom_call" | custom-call | tf_op jit(solution)/shard_map/grad_kv/pallas_call | solution.py:320
  180.7 2.8 %convolution_convert_fusion.5.refs_1_ = bf16[512,768]{1,0:T(8,128)(2,1)} fusion(bf16[768,576]{1,0:T(8,128)(2,1)S(1)} %copy-done.34, bf16[512,384]{1,0:T(8,128)(2,1)} %get-tuple-element.47, bf16[512,192]{1,0:T(8,128)(2,1)S(1)} %copy.65), kind=kOutput, calls=%fused_computation.102 | convolution fusion | flops 454557696 | bytes 2260992 | tf_op jit(solution)/shard_map/dot_general | solution.py:39
  183.8 2.0 convolution_convert_fusion.2
  185.9 0.6 reshape.175.refs_4_
  186.5 1.5 copy.66
  188.0 1.2 pad_maximum_fusion.refs_0_
  189.3 41.9 %grad_first.1 = (f32[192,768]{1,0:T(8,128)}, bf16[512,768]{1,0:T(8,128)(2,1)}, f32[192,768]{1,0:T(8,128)}, f32[192,768]{1,0:T(8,128)}, f32[8,640]{1,0:T(8,128)}) custom-call(bf16[768,768]{1,0:T(8,128)(2,1)} %pad_maximum_fusion.refs_0_, bf16[512,768]{1,0:T(8,128)(2,1)} %convolution_convert_fusion.5.refs_1_, bf16[192,768]{1,0:T(8,128)(2,1)} %get-tuple-element.48.refs_2_, ...), custom_call_target="tpu_custom_call" | custom-call | tf_op jit(solution)/shard_map/grad_first/pallas_call | solution.py:320
  231.2 0.8 reshape.176
  232.0 0.6 fusion.91
  232.6 0.6 slice.142
  233.2 2.1 fusion.42
  235.3 0.6 reshape.177.refs_0_
  235.9 7.5 %gain_sums.1 = f32[8,256]{1,0:T(8,128)} custom-call(f32[8,256]{1,0:T(8,128)} %reshape.177.refs_0_), custom_call_target="tpu_custom_call" | custom-call | tf_op jit(solution)/shard_map/gain_sums/pallas_call | solution.py:320
  243.4 0.7 slice.116
  244.1 0.9 slice_bitcast_fusion
  245.1 0.8 copy.68
  245.9 2.3 add_convert_fusion
  248.2 1.7 fusion.33
  249.9 0.7 constant_dynamic-slice_fusion
  250.6 0.8 copy.78
  251.4 0.8 copy.79
  (114 shorter events, 3.1 us)
Async XLA Ops:
  0.7 4.5 %copy-start.30 = (bf16[192]{0:T(256)(128)(2,1)S(1)}, bf16[192]{0:T(256)(128)(2,1)}, u32[]{:S(2)}) copy-start(bf16[192]{0:T(256)(128)(2,1)} %param.33) | copy-start | bytes 1156
  0.7 4.5 %copy-start.29 = (bf16[192]{0:T(256)(128)(2,1)S(1)}, bf16[192]{0:T(256)(128)(2,1)}, u32[]{:S(2)}) copy-start(bf16[192]{0:T(256)(128)(2,1)} %param.29) | copy-start | bytes 1156
  0.7 4.5 %copy-start.28 = (bf16[192]{0:T(256)(128)(2,1)S(1)}, bf16[192]{0:T(256)(128)(2,1)}, u32[]{:S(2)}) copy-start(bf16[192]{0:T(256)(128)(2,1)} %param.28) | copy-start | bytes 1156
  0.7 4.5 %copy-start.27 = (bf16[192]{0:T(256)(128)(2,1)S(1)}, bf16[192]{0:T(256)(128)(2,1)}, u32[]{:S(2)}) copy-start(bf16[192]{0:T(256)(128)(2,1)} %param.27) | copy-start | bytes 1156
  0.7 4.5 %copy-start.26 = (bf16[192]{0:T(256)(128)(2,1)S(1)}, bf16[192]{0:T(256)(128)(2,1)}, u32[]{:S(2)}) copy-start(bf16[192]{0:T(256)(128)(2,1)} %param.20) | copy-start | bytes 1156
  0.7 4.5 %copy-start.25 = (bf16[192]{0:T(256)(128)(2,1)S(1)}, bf16[192]{0:T(256)(128)(2,1)}, u32[]{:S(2)}) copy-start(bf16[192]{0:T(256)(128)(2,1)} %param.19) | copy-start | bytes 1156
  0.7 5.2 %copy-start.24 = (bf16[768]{0:T(1024)(128)(2,1)S(1)}, bf16[768]{0:T(1024)(128)(2,1)}, u32[]{:S(2)}) copy-start(bf16[768]{0:T(1024)(128)(2,1)} %param.31) | copy-start | bytes 4612
  0.7 5.2 %copy-start.20 = (bf16[192,192]{1,0:T(8,128)(2,1)S(1)}, bf16[192,192]{1,0:T(8,128)(2,1)}, u32[]{:S(2)}) copy-start(bf16[192,192]{1,0:T(8,128)(2,1)} %param.26) | copy-start | bytes 221188
  0.7 5.9 %copy-start.21 = (bf16[192,192]{1,0:T(8,128)(2,1)S(1)}, bf16[192,192]{1,0:T(8,128)(2,1)}, u32[]{:S(2)}) copy-start(bf16[192,192]{1,0:T(8,128)(2,1)} %param.24) | copy-start | bytes 221188
  0.8 5.9 %copy-start.22 = (bf16[192,192]{1,0:T(8,128)(2,1)S(1)}, bf16[192,192]{1,0:T(8,128)(2,1)}, u32[]{:S(2)}) copy-start(bf16[192,192]{1,0:T(8,128)(2,1)} %param.23) | copy-start | bytes 221188
  0.8 5.9 %copy-start.23 = (bf16[192,192]{1,0:T(8,128)(2,1)S(1)}, bf16[192,192]{1,0:T(8,128)(2,1)}, u32[]{:S(2)}) copy-start(bf16[192,192]{1,0:T(8,128)(2,1)} %param.21) | copy-start | bytes 221188
  36.0 2.6 %copy-start.6 = (bf16[1024,768]{1,0:T(8,128)(2,1)S(1)}, bf16[1024,768]{1,0:T(8,128)(2,1)}, u32[]{:S(2)}) copy-start(bf16[1024,768]{1,0:T(8,128)(2,1)} %get-tuple-element.36) | copy-start | bytes 4718596
  36.8 2.8 %copy-start.33 = (bf16[768,576]{1,0:T(8,128)(2,1)S(1)}, bf16[768,576]{1,0:T(8,128)(2,1)}, u32[]{:S(2)}) copy-start(bf16[768,576]{1,0:T(8,128)(2,1)} %get-tuple-element.38) | copy-start | bytes 2654212
  41.0 12.0 %copy-start.7 = (bf16[1024,192]{0,1:T(8,128)(2,1)}, bf16[1024,192]{0,1:T(8,128)(2,1)S(1)}, u32[]{:S(2)}) copy-start(bf16[1024,192]{0,1:T(8,128)(2,1)S(1)} %get-tuple-element.128) | copy-start | bytes 1179652
  47.6 3.4 %copy-start.5 = (bf16[512,768]{1,0:T(8,128)(2,1)S(1)}, bf16[512,768]{1,0:T(8,128)(2,1)}, u32[]{:S(2)}) copy-start(bf16[512,768]{1,0:T(8,128)(2,1)} %refs_3_.1) | copy-start | bytes 2359300
  51.1 28.0 %copy-start.10 = (bf16[768,768]{1,0:T(8,128)(2,1)}, bf16[768,768]{1,0:T(8,128)(2,1)S(1)}, u32[]{:S(2)}) copy-start(bf16[768,768]{1,0:T(8,128)(2,1)S(1)} %reshape.171) | copy-start | bytes 3538948
  54.1 2.7 %copy-start = (f32[3,1024,512]{2,1,0:T(8,128)}, f32[3,1024,512]{2,1,0:T(8,128)S(1)}, u32[]{:S(2)}) copy-start(f32[3,1024,512]{2,1,0:T(8,128)S(1)} %get-tuple-element.147) | copy-start | bytes 18874372
  81.1 8.8 %copy-start.1 = (f32[512,768]{1,0:T(8,128)}, f32[512,768]{1,0:T(8,128)S(1)}, u32[]{:S(2)}) copy-start(f32[512,768]{1,0:T(8,128)S(1)} %get-tuple-element.151) | copy-start | bytes 4718596
  81.1 1.8 copy-start.32
  83.0 4.1 %copy-start.16 = (bf16[512,768]{1,0:T(8,128)(2,1)S(1)}, bf16[512,768]{1,0:T(8,128)(2,1)}, u32[]{:S(2)}) copy-start(bf16[512,768]{1,0:T(8,128)(2,1)} %param.18) | copy-start | bytes 2359300
  83.0 4.1 %copy-start.31 = (bf16[768,768]{1,0:T(8,128)(2,1)S(1)}, bf16[768,768]{1,0:T(8,128)(2,1)}, u32[]{:S(2)}) copy-start(bf16[768,768]{1,0:T(8,128)(2,1)} %get-tuple-element.42) | copy-start | bytes 3538948
  137.1 7.8 %copy-start.15 = (bf16[512,768]{1,0:T(8,128)(2,1)}, bf16[512,768]{1,0:T(8,128)(2,1)S(1)}, u32[]{:S(2)}) copy-start(bf16[512,768]{1,0:T(8,128)(2,1)S(1)} %convolution_convert_fusion.3) | copy-start | bytes 2359300
  138.0 24.9 %collective-permute-start = (bf16[128,768]{1,0:T(8,128)(2,1)}, bf16[128,768]{1,0:T(8,128)(2,1)}, u32[]{:S(2)}, u32[]{:S(2)}) collective-permute-start(bf16[128,768]{1,0:T(8,128)(2,1)} %get-tuple-element.125), channel_id=1, source_target_pairs={{0,1},{1,2},{2,3},{3,0},{4,5},{5,6},{6,7},{7,4},{8,9},{9,10},{10,1... | collective-permute-start | bytes 589832 | tf_op jit(solution)/shard_map/ppermute | solution.py:479
  140.7 22.2 %collective-permute-start.2 = (bf16[128,768]{1,0:T(8,128)(2,1)}, bf16[128,768]{1,0:T(8,128)(2,1)}, u32[]{:S(2)}, u32[]{:S(2)}) collective-permute-start(bf16[128,768]{1,0:T(8,128)(2,1)} %get-tuple-element.126), channel_id=1, source_target_pairs={{0,3},{1,0},{2,1},{3,2},{4,7},{5,4},{6,5},{7,6},{8,11},{9,8},{10,9... | collective-permute-start | bytes 589832 | tf_op jit(solution)/shard_map/ppermute | solution.py:479
  141.8 21.1 %collective-permute-start.1 = (bf16[128,768]{1,0:T(8,128)(2,1)}, bf16[128,768]{1,0:T(8,128)(2,1)}, u32[]{:S(2)}, u32[]{:S(2)}) collective-permute-start(bf16[128,768]{1,0:T(8,128)(2,1)} %get-tuple-element.127), channel_id=1, source_target_pairs={{0,2},{1,3},{2,0},{3,1},{4,6},{5,7},{6,4},{7,5},{8,10},{9,11},{10,... | collective-permute-start | bytes 589832 | tf_op jit(solution)/shard_map/ppermute | solution.py:479
  144.8 11.9 %slice-start = ((s8[6291456]{0:T(1024)(128)(4,1)}), s8[2097152]{0:T(1024)(128)(4,1)S(1)}, s32[]{:S(2)}) async-start(s8[6291456]{0:T(1024)(128)(4,1)} %bitcast.114), calls=%async_computation | async-start | bytes 4194304
  150.0 10.3 %copy-start.3 = (f32[512,768]{1,0:T(8,128)}, f32[512,768]{1,0:T(8,128)S(1)}, u32[]{:S(2)}) copy-start(f32[512,768]{1,0:T(8,128)S(1)} %get-tuple-element.121) | copy-start | bytes 4718596
  150.0 1.8 copy-start.12
  150.0 6.8 %slice-start.1 = ((s8[6291456]{0:T(1024)(128)(4,1)}), s8[4194304]{0:T(1024)(128)(4,1)S(1)}, s32[]{:S(2)}) async-start(s8[6291456]{0:T(1024)(128)(4,1)} %bitcast.114), calls=%async_computation.1 | async-start | bytes 8388608
  156.8 1.8 copy-start.8
  159.2 1.1 copy-start.11
  160.3 1.0 copy-start.13
  161.7 19.0 %copy-start.34 = (bf16[768,576]{1,0:T(8,128)(2,1)S(1)}, bf16[768,576]{1,0:T(8,128)(2,1)}, u32[]{:S(2)}) copy-start(bf16[768,576]{1,0:T(8,128)(2,1)} %get-tuple-element.38) | copy-start | bytes 2654212
  180.7 2.8 %copy-start.19 = (bf16[512,384]{1,0:T(8,128)(2,1)S(1)}, bf16[512,384]{1,0:T(8,128)(2,1)}, u32[]{:S(2)}) copy-start(bf16[512,384]{1,0:T(8,128)(2,1)} %get-tuple-element.47) | copy-start | bytes 1179652
  231.2 12.9 %copy-start.14 = (f32[192,768]{1,0:T(8,128)S(1)}, f32[192,768]{1,0:T(8,128)}, u32[]{:S(2)}) copy-start(f32[192,768]{1,0:T(8,128)} %get-tuple-element.52) | copy-start | bytes 1769476
  233.2 12.6 %copy-start.2 = (f32[512,768]{1,0:T(8,128)S(1)}, f32[512,768]{1,0:T(8,128)}, u32[]{:S(2)}) copy-start(f32[512,768]{1,0:T(8,128)} %copy-done.1) | copy-start | bytes 4718596
  245.9 2.4 copy-start.4
  245.9 2.4 copy-start.9
  248.2 2.4 copy-start.18
  249.9 1.5 copy-start.17

commit v4 on v3

--- a/solution.py
+++ b/solution.py
@@ -199,6 +199,33 @@
     finish(backs)
 
 
+def reduce_stat_steps(
+    axes, sizes, more_axes, more_sizes, src, normed, out, stats,
+    landing, part, near_sum, near_held, far_held, sems, back_sems, near_sems, far_sems,
+):
+    rows = landing.shape[1]
+    mine, copies = deal(src, landing, rows, axes, sizes, sems)
+    yield
+    total = src[rows_at(mine, rows), :].astype(F32)
+    for slot, copy in enumerate(copies):
+        copy.wait_recv()
+        total = total + landing[slot].astype(F32)
+    low = total.astype(out.dtype)
+    block = rows_at(mine, rows)
+    out[block, :] = low
+    _, backs = spread(out.at[block], out, rows, axes, sizes, back_sems)
+    low = low.astype(F32)
+    part[...] = jnp.zeros_like(part)
+    part[0:1, :] = jnp.sum(low * normed[...], axis=0, keepdims=True)
+    part[1:2, :] = jnp.sum(low, axis=0, keepdims=True)
+    yield from share_steps(axes, sizes, part, near_sum, near_held, near_sems)
+    yield from share_steps(more_axes, more_sizes, near_sum, stats, far_held, far_sems)
+    for copy in backs:
+        copy.wait_recv()
+    finish(copies)
+    finish(backs)
+
+
 def sum_blocks(held, rows, count):
     total = held[0:rows, :].astype(F32)
     for index in range(1, count):
@@ -225,7 +252,7 @@
 
 
 def plan_of(kind, axes, sizes, more, array, out_type):
-    rows, cols = array.shape
+    rows, cols = (array[0] if kind == "reduce_stat" else array).shape
     count = 1
     for size in sizes:
         count *= size
@@ -249,6 +276,27 @@
                 pltpu.SemaphoreType.DMA((2, more_count - 1)),
             ],
             functools.partial(chain_steps, axes, sizes, more_axes, more_sizes),
+        )
+    if kind == "reduce_stat":
+        more_axes, more_sizes = more
+        more_count = 1
+        for size in more_sizes:
+            more_count *= size
+        small = pltpu.VMEM((8, cols), F32)
+        return (
+            [(rows, cols), (8, cols)],
+            [
+                pltpu.VMEM((peers, rows // count, cols), array[0].dtype),
+                small,
+                small,
+                pltpu.VMEM((count * 8, cols), F32),
+                pltpu.VMEM((more_count * 8, cols), F32),
+                pair,
+                pair,
+                pair,
+                pltpu.SemaphoreType.DMA((2, more_count - 1)),
+            ],
+            functools.partial(reduce_stat_steps, axes, sizes, more_axes, more_sizes),
         )
     block = rows // count
     one = pltpu.VMEM((block, cols), array.dtype)
@@ -297,11 +345,22 @@
         for offset in offsets(sized(group)):
             key = tuple(sorted((a, o) for a, o in zip(group, offset) if o))
             places.setdefault(key, (group, offset))
-    count = len(jobs)
+    in_counts = [len(job[2]) if isinstance(job[2], tuple) else 1 for job in jobs]
+    arrays = []
+    shapes = []
+    out_counts = []
+    for job, plan in zip(jobs, plans):
+        arrays.extend(job[2] if isinstance(job[2], tuple) else (job[2],))
+        many = isinstance(plan[0], list)
+        outs = zip(plan[0], job[3]) if many else [(plan[0], job[3])]
+        outs = [jax.ShapeDtypeStruct(shape, kind) for shape, kind in outs]
+        shapes.extend(outs)
+        out_counts.append(len(outs))
 
     def kernel(*refs):
-        sources, outs = refs[:count], refs[count : 2 * count]
-        scratch = list(refs[2 * count :])
+        sources = list(refs[: len(arrays)])
+        outs = list(refs[len(arrays) : len(arrays) + len(shapes)])
+        scratch = list(refs[len(arrays) + len(shapes) :])
         barrier = pltpu.get_barrier_semaphore()
         for group, offset in places.values():
             place, _ = group_place(group, sized(group), offset)
@@ -310,9 +369,10 @@
             )
         pl.semaphore_wait(barrier, len(places))
         running = []
-        for source, out, (_, needs, steps) in zip(sources, outs, plans):
+        for ins, made, (_, needs, steps) in zip(in_counts, out_counts, plans):
             mine, scratch = scratch[: len(needs)], scratch[len(needs) :]
-            running.append(steps(source, out, *mine))
+            running.append(steps(*sources[:ins], *outs[:made], *mine))
+            sources, outs = sources[ins:], outs[made:]
         while running:
             running = [step for step in running if next(step, "end") != "end"]
 
@@ -320,18 +380,16 @@
     return pl.pallas_call(
         kernel,
         name=name,
-        out_shape=[
-            jax.ShapeDtypeStruct(plan[0], job[3]) for plan, job in zip(plans, jobs)
-        ],
-        in_specs=[whole] * count,
-        out_specs=[whole] * count,
+        out_shape=shapes,
+        in_specs=[whole] * len(arrays),
+        out_specs=[whole] * len(shapes),
         scratch_shapes=[need for plan in plans for need in plan[1]],
         compiler_params=pltpu.CompilerParams(
             collective_id=collective_id,
             has_side_effects=True,
             vmem_limit_bytes=56 * 1024 * 1024,
         ),
-    )(*[job[2] for job in jobs])
+    )(*arrays)
 
 
 def pack_vectors(vectors):
@@ -382,8 +440,6 @@
     )
     wide = -(-flat.shape[0] // (16 * 128)) * 128
     vectors = jnp.pad(flat, (0, 16 * wide - flat.shape[0])).reshape(16, wide)
-    half = local_width // 2
-    out_packed = jnp.concatenate([out_weight[:half], out_weight[half:]], axis=1)
     attn_weights = jnp.concatenate([query_weight, key_weight, value_weight], axis=1)
     qkv_full, vectors_full, out_blocks, frames_all = transfers(
         1,
@@ -391,7 +447,7 @@
         [
             ("gather", ("clip",), attn_weights, BF16),
             ("gather", ("clip",), vectors, BF16),
-            ("chain", ("tp",), out_packed, BF16, ("clip",)),
+            ("chain", ("tp",), out_weight, BF16, ("clip",)),
             ("gather", ("ctx",), frames, BF16),
         ],
     )
@@ -402,9 +458,8 @@
     ]
     kv_full = qkv_full[:, local_width:]
     query_full = qkv_full[:, :local_width]
-    groups = width // local_width
-    out_blocks = out_blocks.reshape(clips, groups, half, 2, share)
-    out_all = out_blocks.transpose(1, 3, 2, 0, 4).reshape(width, width)
+    out_blocks = out_blocks.reshape(clips, width, share)
+    out_all = out_blocks.transpose(1, 0, 2).reshape(width, width)
     out_rows = lax.dynamic_slice_in_dim(out_all, lax.axis_index("tp") * local_width, local_width)
     inputs = frames.astype(F32)
     normed_one, factor_one = center_rows(inputs)
@@ -526,27 +581,29 @@
         qkv_bias[:local_width],
         qkv_bias[2 * local_width :],
     ]
-    sum_attn, grad_first, sum_expand, sum_reduce_t, early_sum = transfers(
+    normed_part = lax.dynamic_slice_in_dim(normed_one, tp_at * part_rows, part_rows)
+    sum_attn, grad_first, late_sum, sum_expand, sum_reduce_t, early_sum = transfers(
         5,
         "grad_first",
         [
             ("both", ("clip",), grad_attn_weights, F32, ("ctx",)),
-            ("reduce", ("tp",), first_terms, BF16),
+            (
+                "reduce_stat",
+                ("tp",),
+                (first_terms, normed_part),
+                (BF16, F32),
+                ("clip", "ctx"),
+            ),
             ("share", ("ctx",), share_expand, F32),
             ("share", ("ctx",), share_reduce_t, F32),
             ("share", ("clip", "ctx"), pack_vectors(early), F32),
         ],
     )
     grad_first = grad_first.astype(F32)
-    late = [jnp.sum(grad_first * normed_one, axis=0), jnp.sum(grad_first, axis=0)]
-    (late_sum,) = transfers(
-        6, "gain_sums", [("share", ("clip", "ctx"), pack_vectors(late), F32)]
-    )
     frames_grad = grad_hidden + norm_back(grad_first, normed_one, factor_one, gain_first)
 
     sums = unpack_vectors(early_sum, [4 * width, hidden_width, local_width, local_width])
-    (late_sums,) = unpack_vectors(late_sum, [2 * width])
-    shared = jnp.concatenate([sums[0], late_sums]).reshape(6, width)
+    shared = jnp.concatenate([sums[0].reshape(4, width), late_sum[:2]])
     shared = lax.dynamic_slice(shared, (0, clip_at), (6, share))
     return (
         layer_out,

time: 257 us -> 259 us (level); the launches traced: 252 us -> 258 us
  matrix products: 35.4 us -> 40.4 us
  Pallas kernels: 156 us -> 159 us
    reshape x4 -> x2, local copies, waits for them, and re-layouts: 9.85 us -> 1.46 us  [the longest x1 1.45 us: shards(): out_blocks = out_blocks.reshape(clips, width, share)]
    concatenate x1, local copies, waits for them, and re-layouts: 0.09 us -> 4.09 us  [shards(): jnp.concatenate([first_gain, first_shift, out_bias, second_gain, second_s...]
    pallas_call x6 -> x5, Pallas kernels: 156 us -> 159 us  [transfers(): pl.pallas_call(kernel, name=name, out_shape=shapes, in_specs=[whole] * le...]
    unnamed x77 -> x71, local copies, waits for them, and re-layouts: 5.95 us -> 5.97 us
  transfers between devices with their start and end apart: 3 -> 3, of which waited for: 0 -> 0; matrix products, arithmetic and copies ran while one was open for 7% -> 10% of each run, Pallas kernels for 0% -> 0%
where the time goes in v4:
time: 259 us; the launch traced here: 258 us
  Pallas kernels  159 us (61%)
  matrix products  40.4 us (16%)
  local copies, waits for them, and re-layouts  26 us (10%)
  other arithmetic  25 us (10%)
  starting transfers between devices  6.16 us (2%)
    pallas_call x5, Pallas kernels, transfers(): pl.pallas_call(kernel, name=name, out_shape=shapes, in_specs=[whole] * le...  159 us
    dot_general x4, matrix products, product(): return jnp.dot(left, right, preferred_element_type=jnp.float32)  10.5 us
    dot_general x5, matrix products, rows_inner(): lax.dot_general(left, right, (((0,), (0,)), ((), ())), preferred_element_...  10.5 us
    dot_general x4, matrix products, cols_inner(): lax.dot_general(left, right, (((1,), (1,)), ((), ())), preferred_element_...  7.53 us
    ppermute x3, starting transfers between devices, shards(): lax.ppermute(mlp_block((tp_at + step) % tp_size), 'tp', ring)  6.16 us
    unnamed x71, local copies, waits for them, and re-layouts  5.97 us
  transfers between devices with their start and end apart: 3, of which 0 were waited for; matrix products, arithmetic and copies ran while one was open for 10% of the time, Pallas kernels for 0%

profile of v4, /device:TPU:0, one launch (start us, length us, event | category | flops | bytes accessed | tf_op | source)
XLA Modules:
  0.0 257.8 jit_solution(8644239906099921871)
XLA Ops:
  0.7 4.1 %concatenate.26 = bf16[1152]{0:T(1024)(128)(2,1)S(1)} concatenate(bf16[192]{0:T(256)(128)(2,1)} %param.19, bf16[192]{0:T(256)(128)(2,1)} %param.20, bf16[192]{0:T(256)(128)(2,1)} %param.27, bf16[192]{0:T(256)(128)(2,1)} %param.28, bf16[192]{0:T(256)(128)(2,1)} %param.29, bf16[192]{0:T(256)(128)(2,1)} %param.33), dimensions={0} | concatenate | bytes 4608 | tf_op jit(solution)/shard_map/concatenate | solution.py:438
  4.7 0.6 pad_bitcast_fusion.refs_1_
  5.3 1.3 convert_reduce_fusion.2
  6.7 1.8 pad_maximum_fusion.3.refs_0_
  8.4 28.8 %gather_first.1 = (bf16[768,576]{1,0:T(8,128)(2,1)}, bf16[64,128]{1,0:T(8,128)(2,1)}, bf16[3072,192]{1,0:T(8,128)(2,1)}, bf16[1024,768]{1,0:T(8,128)(2,1)}) custom-call(bf16[192,576]{1,0:T(8,128)(2,1)} %pad_maximum_fusion.3.refs_0_, bf16[16,128]{1,0:T(8,128)(2,1)} %pad_bitcast_fusion.refs_1_, bf16[192,192]{1,0:T(8,128)(2,1)} %refs_2_.1, bf16[512,768]{1,0:T(8,128)(2,1)} %refs_3_.1), custom_call_target="tpu_custom_call" | custom-call | tf_op jit(solution)/shard_map/gather_first/pallas_call | solution.py:380
  37.2 0.8 reshape.161
  38.3 1.8 convert_reduce_fusion
  40.1 0.6 fusion.9
  40.9 1.3 add_convert_fusion.3
  42.3 1.2 copy-done.1
  43.5 0.4 fusion.24
  44.0 1.4 copy.58
  45.5 1.6 fusion.61
  47.1 1.0 bitcast_reduce_fusion
  48.1 1.0 fusion.5
  49.2 1.6 copy-done
  50.8 1.9 fusion.83
  52.8 20.9 %gather_mixed.1 = (bf16[768,768]{1,0:T(8,128)(2,1)}, bf16[768,768]{1,0:T(8,128)(2,1)}, bf16[768,512]{1,0:T(8,128)(2,1)}) custom-call(bf16[192,768]{1,0:T(8,128)(2,1)} %refs_0_.1, bf16[192,768]{1,0:T(8,128)(2,1)} %bitcast.134, bf16[192,512]{1,0:T(8,128)(2,1)} %bitcast.125), custom_call_target="tpu_custom_call" | custom-call | tf_op jit(solution)/shard_map/gather_mixed/pallas_call | solution.py:380
  73.7 2.0 fusion.84
  75.8 0.3 multiply_reduce_fusion.1
  76.5 6.5 %multiply_convert_fusion = (bf16[512,768]{1,0:T(8,128)(2,1)}, f32[512,768]{1,0:T(8,128)S(1)}, f32[512,768]{1,0:T(8,128)S(1)}) fusion(f32[768]{0:T(1024)S(1)} %convert_element_type.162, bf16[768,768]{1,0:T(8,128)(2,1)} %get-tuple-element.42, f32[512,768]{1,0:T(8,128)S(1)} %get-tuple-element.149, f32[768]{0:T(1024)S(1)} %add.189, f32[768]{0:T(1024)S(1)} %mul.204, ...), kind=kOutput, calls=%fused_computation.61 | convolution fusion | flops 631898112 | bytes 6697984 | tf_op jit(solution)/shard_map/dot_general | solution.py:29
  82.9 1.2 convert_reduce_fusion.4
  84.2 1.7 convolution_convert_fusion.4.refs_2_
  85.9 2.1 convolution_convert_fusion.1.refs_0_
  88.0 3.3 %fusion.50.refs_1_ = bf16[768,768]{1,0:T(8,128)(2,1)} fusion(bf16[512,768]{1,0:T(8,128)(2,1)} %get-tuple-element.46, bf16[512,768]{1,0:T(8,128)(2,1)} %param.18), kind=kOutput, calls=%fused_computation.88 | convolution fusion | flops 604569600 | bytes 2752512 | tf_op jit(solution)/shard_map/dot_general | solution.py:33
  91.2 40.1 %grad_second.1 = (bf16[192,768]{1,0:T(8,128)(2,1)}, bf16[192,768]{1,0:T(8,128)(2,1)}, bf16[512,768]{1,0:T(8,128)(2,1)}) custom-call(bf16[768,768]{1,0:T(8,128)(2,1)} %convolution_convert_fusion.1.refs_0_, bf16[768,768]{1,0:T(8,128)(2,1)} %fusion.50.refs_1_, bf16[512,768]{1,0:T(8,128)(2,1)} %convolution_convert_fusion.4.refs_2_), custom_call_target="tpu_custom_call" | custom-call | tf_op jit(solution)/shard_map/grad_second/pallas_call | solution.py:380
  131.3 0.8 convolution_convert_fusion.3
  132.2 0.8 constant_dynamic-slice_fusion.3
  133.0 3.8 %collective-permute-start = (bf16[128,768]{1,0:T(8,128)(2,1)}, bf16[128,768]{1,0:T(8,128)(2,1)}, u32[]{:S(2)}, u32[]{:S(2)}) collective-permute-start(bf16[128,768]{1,0:T(8,128)(2,1)} %get-tuple-element.125), channel_id=1, source_target_pairs={{0,1},{1,2},{2,3},{3,0},{4,5},{5,6},{6,7},{7,4},{8,9},{9,10},{10,1... | collective-permute-start | bytes 589832 | tf_op jit(solution)/shard_map/ppermute | solution.py:534
  136.8 2.3 collective-permute-start.1
  139.2 1.5 fusion.22
  140.7 0.8 fusion.30
  141.5 3.7 %convert_reduce_fusion.5 = (f32[768]{0:T(1024)S(1)}, f32[512,768]{1,0:T(8,128)}, f32[768]{0:T(1024)S(1)}) fusion(f32[512]{0:T(512)S(1)} %get-tuple-element.153, f32[512,768]{1,0:T(8,128)} %copy-done.2, f32[512]{0:T(512)S(1)} %broadcast_multiply_fusion.5, f32[512]{0:T(512)S(1)} %get-tuple-element.154, f32[768]{0:T(1024)S(1)} %mul.204, ...), kind=kLoop, calls=%fused_computation.59 | loop fusion | flops 5503488 | bytes 4736000 | tf_op jit(solution)/shard_map/reduce_sum | solution.py:579
  145.3 2.2 convolution_convert_fusion.7
  147.6 4.7 %fusion.54 = bf16[3,64,1024]{2,1,0:T(8,128)(2,1)} fusion(bf16[512,3,64]{0,2,1:T(8,128)(2,1)S(1)} %bitcast.121, f32[3,1024,512]{2,1,0:T(8,128)} %copy-done, f32[512,3]{0,1:T(4,128)S(1)} %log_add_fusion), kind=kOutput, calls=%fused_computation.95 | convolution fusion | flops 206241792 | bytes 6887424 | tf_op jit(solution)/shard_map/qhk,qhd->khd/dot_general | solution.py:548
  152.3 1.8 fusion.1
  154.1 1.1 fusion.53
  155.2 1.3 fusion.60
  156.6 1.0 convolution_convert_fusion.6
  157.9 1.2 copy.63
  159.1 1.8 copy.65
  160.8 1.9 copy.67
  162.8 1.2 pad_maximum_fusion.1.refs_0_
  164.0 2.3 add_convert_fusion.4
  166.3 18.2 %grad_kv.1 = (bf16[512,384]{1,0:T(8,128)(2,1)}, bf16[512,768]{1,0:T(8,128)(2,1)}) custom-call(bf16[1024,384]{1,0:T(8,128)(2,1)} %pad_maximum_fusion.1.refs_0_, bf16[128,768]{1,0:T(8,128)(2,1)} %get-tuple-element.155.refs_1_), custom_call_target="tpu_custom_call" | custom-call | tf_op jit(solution)/shard_map/grad_kv/pallas_call | solution.py:380
  184.5 1.3 convert_reduce_fusion.6
  185.8 2.8 %convolution_convert_fusion.5.refs_1_ = bf16[512,768]{1,0:T(8,128)(2,1)} fusion(bf16[768,576]{1,0:T(8,128)(2,1)S(1)} %copy-done.29, bf16[512,384]{1,0:T(8,128)(2,1)} %get-tuple-element.48, bf16[512,192]{1,0:T(8,128)(2,1)S(1)} %copy-done.16), kind=kOutput, calls=%fused_computation.91 | convolution fusion | flops 454557696 | bytes 2260992 | tf_op jit(solution)/shard_map/dot_general | solution.py:39
  188.6 2.0 convolution_convert_fusion.2
  190.7 0.6 reshape.170.refs_5_
  191.3 1.5 copy.66
  192.8 2.2 pad_maximum_fusion.refs_0_
  195.1 51.1 %grad_first.1 = (f32[192,768]{1,0:T(8,128)}, bf16[512,768]{1,0:T(8,128)(2,1)}, f32[8,768]{1,0:T(8,128)}, f32[192,768]{1,0:T(8,128)}, f32[192,768]{1,0:T(8,128)}, /*index=5*/f32[8,640]{1,0:T(8,128)}) custom-call(bf16[768,768]{1,0:T(8,128)(2,1)} %pad_maximum_fusion.refs_0_, bf16[512,768]{1,0:T(8,128)(2,1)} %convolution_convert_fusion.5.refs_1_, ...), custom_call_target="tpu_custom_call" | custom-call | tf_op jit(solution)/shard_map/grad_first/pallas_call | solution.py:380
  246.2 0.7 reshape.171
  246.9 0.6 slice.135
  247.5 0.6 fusion.80
  248.2 0.8 slice.104
  249.1 0.6 fusion.81
  249.7 1.8 fusion.40
  251.5 0.9 slice_bitcast_fusion
  252.4 0.8 copy.68
  253.2 1.7 multiply_add_fusion
  255.1 1.1 add_convert_fusion
  256.2 0.8 copy.76
  257.0 0.8 copy.77
  (102 shorter events, 2.1 us)
Async XLA Ops:
  37.2 2.9 %copy-start.6 = (bf16[1024,768]{1,0:T(8,128)(2,1)S(1)}, bf16[1024,768]{1,0:T(8,128)(2,1)}, u32[]{:S(2)}) copy-start(bf16[1024,768]{1,0:T(8,128)(2,1)} %get-tuple-element.37) | copy-start | bytes 4718596
  38.3 2.5 copy-start.24
  38.3 2.6 copy-start.28
  42.2 1.3 copy-start.1
  42.2 1.6 copy-start.30
  42.2 1.8 copy-start.14
  42.3 4.8 %copy-start.7 = (bf16[1024,192]{0,1:T(8,128)(2,1)}, bf16[1024,192]{0,1:T(8,128)(2,1)S(1)}, u32[]{:S(2)}) copy-start(bf16[1024,192]{0,1:T(8,128)(2,1)S(1)} %get-tuple-element.128) | copy-start | bytes 1179652
  48.1 2.7 %copy-start = (f32[3,1024,512]{2,1,0:T(8,128)}, f32[3,1024,512]{2,1,0:T(8,128)S(1)}, u32[]{:S(2)}) copy-start(f32[3,1024,512]{2,1,0:T(8,128)S(1)} %get-tuple-element.145) | copy-start | bytes 18874372
  50.8 22.9 %copy-start.11 = (bf16[4,768,192]{1,2,0:T(8,128)(2,1)S(1)}, bf16[4,768,192]{1,2,0:T(8,128)(2,1)}, u32[]{:S(2)}) copy-start(bf16[4,768,192]{1,2,0:T(8,128)(2,1)} %copy.58) | copy-start | bytes 3538948
  75.8 10.1 %copy-start.2 = (f32[512,768]{1,0:T(8,128)}, f32[512,768]{1,0:T(8,128)S(1)}, u32[]{:S(2)}) copy-start(f32[512,768]{1,0:T(8,128)S(1)} %get-tuple-element.149) | copy-start | bytes 4718596
  75.8 0.7 copy-start.23
  76.5 6.5 %copy-start.19 = (bf16[512,768]{1,0:T(8,128)(2,1)S(1)}, bf16[512,768]{1,0:T(8,128)(2,1)}, u32[]{:S(2)}) copy-start(bf16[512,768]{1,0:T(8,128)(2,1)} %param.18) | copy-start | bytes 2359300
  76.5 6.5 %copy-start.25 = (bf16[768,768]{1,0:T(8,128)(2,1)S(1)}, bf16[768,768]{1,0:T(8,128)(2,1)}, u32[]{:S(2)}) copy-start(bf16[768,768]{1,0:T(8,128)(2,1)} %get-tuple-element.43) | copy-start | bytes 3538948
  82.9 1.3 copy-start.27
  91.2 40.1 %copy-start.26 = (bf16[768,768]{1,0:T(8,128)(2,1)S(1)}, bf16[768,768]{1,0:T(8,128)(2,1)}, u32[]{:S(2)}) copy-start(bf16[768,768]{1,0:T(8,128)(2,1)} %get-tuple-element.43) | copy-start | bytes 3538948
  91.2 40.1 %copy-start.31 = (bf16[512,768]{1,0:T(8,128)(2,1)S(1)}, bf16[512,768]{1,0:T(8,128)(2,1)}, u32[]{:S(2)}) copy-start(bf16[512,768]{1,0:T(8,128)(2,1)} %get-tuple-element.46) | copy-start | bytes 2359300
  132.2 8.5 %copy-start.17 = (bf16[512,768]{1,0:T(8,128)(2,1)}, bf16[512,768]{1,0:T(8,128)(2,1)S(1)}, u32[]{:S(2)}) copy-start(bf16[512,768]{1,0:T(8,128)(2,1)S(1)} %convolution_convert_fusion.3) | copy-start | bytes 2359300
  132.2 8.5 %copy-start.3 = (f32[512,768]{1,0:T(8,128)S(1)}, f32[512,768]{1,0:T(8,128)}, u32[]{:S(2)}) copy-start(f32[512,768]{1,0:T(8,128)} %copy-done.2) | copy-start | bytes 4718596
  132.2 8.5 %copy-start.10 = (bf16[512,768]{1,0:T(8,128)(2,1)S(1)}, bf16[512,768]{1,0:T(8,128)(2,1)}, u32[]{:S(2)}) copy-start(bf16[512,768]{1,0:T(8,128)(2,1)} %get-tuple-element.45) | copy-start | bytes 2359300
  133.0 30.9 %collective-permute-start = (bf16[128,768]{1,0:T(8,128)(2,1)}, bf16[128,768]{1,0:T(8,128)(2,1)}, u32[]{:S(2)}, u32[]{:S(2)}) collective-permute-start(bf16[128,768]{1,0:T(8,128)(2,1)} %get-tuple-element.125), channel_id=1, source_target_pairs={{0,1},{1,2},{2,3},{3,0},{4,5},{5,6},{6,7},{7,4},{8,9},{9,10},{10,1... | collective-permute-start | bytes 589832 | tf_op jit(solution)/shard_map/ppermute | solution.py:534
  136.8 27.1 %collective-permute-start.1 = (bf16[128,768]{1,0:T(8,128)(2,1)}, bf16[128,768]{1,0:T(8,128)(2,1)}, u32[]{:S(2)}, u32[]{:S(2)}) collective-permute-start(bf16[128,768]{1,0:T(8,128)(2,1)} %get-tuple-element.127), channel_id=1, source_target_pairs={{0,2},{1,3},{2,0},{3,1},{4,6},{5,7},{6,4},{7,5},{8,10},{9,11},{10,... | collective-permute-start | bytes 589832 | tf_op jit(solution)/shard_map/ppermute | solution.py:534
  139.1 24.9 %collective-permute-start.2 = (bf16[128,768]{1,0:T(8,128)(2,1)}, bf16[128,768]{1,0:T(8,128)(2,1)}, u32[]{:S(2)}, u32[]{:S(2)}) collective-permute-start(bf16[128,768]{1,0:T(8,128)(2,1)} %get-tuple-element.126), channel_id=1, source_target_pairs={{0,3},{1,0},{2,1},{3,2},{4,7},{5,4},{6,5},{7,6},{8,11},{9,8},{10,9... | collective-permute-start | bytes 589832 | tf_op jit(solution)/shard_map/ppermute | solution.py:534
  140.7 11.6 %slice-start = ((s8[6291456]{0:T(1024)(128)(4,1)}), s8[2097152]{0:T(1024)(128)(4,1)S(1)}, s32[]{:S(2)}) async-start(s8[6291456]{0:T(1024)(128)(4,1)} %bitcast.114), calls=%async_computation | async-start | bytes 4194304
  145.3 2.3 copy-start.13
  145.3 7.1 %slice-start.1 = ((s8[6291456]{0:T(1024)(128)(4,1)}), s8[4194304]{0:T(1024)(128)(4,1)S(1)}, s32[]{:S(2)}) async-start(s8[6291456]{0:T(1024)(128)(4,1)} %bitcast.114), calls=%async_computation.1 | async-start | bytes 8388608
  154.1 1.1 copy-start.8
  155.2 1.4 copy-start.5
  155.2 1.4 copy-start.12
  164.0 20.5 %copy-start.16 = (bf16[512,192]{1,0:T(8,128)(2,1)S(1)}, bf16[512,192]{1,0:T(8,128)(2,1)}, u32[]{:S(2)}) copy-start(bf16[512,192]{1,0:T(8,128)(2,1)} %copy.65) | copy-start | bytes 589828
  164.0 21.8 %copy-start.29 = (bf16[768,576]{1,0:T(8,128)(2,1)S(1)}, bf16[768,576]{1,0:T(8,128)(2,1)}, u32[]{:S(2)}) copy-start(bf16[768,576]{1,0:T(8,128)(2,1)} %get-tuple-element.39) | copy-start | bytes 2654212
  185.8 2.8 %copy-start.22 = (bf16[512,384]{1,0:T(8,128)(2,1)S(1)}, bf16[512,384]{1,0:T(8,128)(2,1)}, u32[]{:S(2)}) copy-start(bf16[512,384]{1,0:T(8,128)(2,1)} %get-tuple-element.48) | copy-start | bytes 1179652
  248.2 3.3 %copy-start.15 = (f32[192,768]{1,0:T(8,128)S(1)}, f32[192,768]{1,0:T(8,128)}, u32[]{:S(2)}) copy-start(f32[192,768]{1,0:T(8,128)} %get-tuple-element.54) | copy-start | bytes 1769476
  249.7 3.6 %copy-start.9 = (bf16[512,768]{1,0:T(8,128)(2,1)S(1)}, bf16[512,768]{1,0:T(8,128)(2,1)}, u32[]{:S(2)}) copy-start(bf16[512,768]{1,0:T(8,128)(2,1)} %get-tuple-element.51) | copy-start | bytes 2359300
  253.2 1.7 copy-start.4
  253.2 1.9 copy-start.18
  255.1 1.1 copy-start.21
  255.1 1.9 copy-start.20

commit v5 on v4

--- a/solution.py
+++ b/solution.py
@@ -210,15 +210,17 @@
     for slot, copy in enumerate(copies):
         copy.wait_recv()
         total = total + landing[slot].astype(F32)
-    low = total.astype(out.dtype)
     block = rows_at(mine, rows)
-    out[block, :] = low
-    _, backs = spread(out.at[block], out, rows, axes, sizes, back_sems)
-    low = low.astype(F32)
+    out[block, :] = total.astype(out.dtype)
+    low = out[block, :].astype(F32)
     part[...] = jnp.zeros_like(part)
     part[0:1, :] = jnp.sum(low * normed[...], axis=0, keepdims=True)
     part[1:2, :] = jnp.sum(low, axis=0, keepdims=True)
-    yield from share_steps(axes, sizes, part, near_sum, near_held, near_sems)
+    near = share_steps(axes, sizes, part, near_sum, near_held, near_sems)
+    next(near)
+    _, backs = spread(out.at[block], out, rows, axes, sizes, back_sems)
+    yield
+    next(near, None)
     yield from share_steps(more_axes, more_sizes, near_sum, stats, far_held, far_sems)
     for copy in backs:
         copy.wait_recv()

time: 259 us -> 253 us (0.977)
  Pallas kernels: 159 us -> 153 us
    pallas_call x5, Pallas kernels: 159 us -> 153 us  [transfers(): pl.pallas_call(kernel, name=name, out_shape=shapes, in_specs=[whole] * le...]
where the time goes in v5:
time: 253 us; the launch traced here: 251 us
  Pallas kernels  153 us (60%)
  matrix products  40.4 us (16%)
  local copies, waits for them, and re-layouts  26 us (10%)
  other arithmetic  25 us (10%)
  starting transfers between devices  6.16 us (2%)
    pallas_call x5, Pallas kernels, transfers(): pl.pallas_call(kernel, name=name, out_shape=shapes, in_specs=[whole] * le...  153 us
    dot_general x4, matrix products, product(): return jnp.dot(left, right, preferred_element_type=jnp.float32)  10.5 us
    dot_general x5, matrix products, rows_inner(): lax.dot_general(left, right, (((0,), (0,)), ((), ())), preferred_element_...  10.5 us
    dot_general x4, matrix products, cols_inner(): lax.dot_general(left, right, (((1,), (1,)), ((), ())), preferred_element_...  7.53 us
    ppermute x3, starting transfers between devices, shards(): lax.ppermute(mlp_block((tp_at + step) % tp_size), 'tp', ring)  6.16 us
    unnamed x71, local copies, waits for them, and re-layouts  5.97 us
  transfers between devices with their start and end apart: 3, of which 0 were waited for; matrix products, arithmetic and copies ran while one was open for 10% of the time, Pallas kernels for 0%

profile of v5, /device:TPU:0, one launch (start us, length us, event | category | flops | bytes accessed | tf_op | source)
XLA Modules:
  0.0 251.3 jit_solution(11898558267646679075)
XLA Ops:
  0.7 4.1 %concatenate.26 = bf16[1152]{0:T(1024)(128)(2,1)S(1)} concatenate(bf16[192]{0:T(256)(128)(2,1)} %param.19, bf16[192]{0:T(256)(128)(2,1)} %param.20, bf16[192]{0:T(256)(128)(2,1)} %param.27, bf16[192]{0:T(256)(128)(2,1)} %param.28, bf16[192]{0:T(256)(128)(2,1)} %param.29, bf16[192]{0:T(256)(128)(2,1)} %param.33), dimensions={0} | concatenate | bytes 4608 | tf_op jit(solution)/shard_map/concatenate | solution.py:440
  4.7 0.6 pad_bitcast_fusion.refs_1_
  5.3 1.3 convert_reduce_fusion.2
  6.7 1.8 pad_maximum_fusion.3.refs_0_
  8.4 28.8 %gather_first.1 = (bf16[768,576]{1,0:T(8,128)(2,1)}, bf16[64,128]{1,0:T(8,128)(2,1)}, bf16[3072,192]{1,0:T(8,128)(2,1)}, bf16[1024,768]{1,0:T(8,128)(2,1)}) custom-call(bf16[192,576]{1,0:T(8,128)(2,1)} %pad_maximum_fusion.3.refs_0_, bf16[16,128]{1,0:T(8,128)(2,1)} %pad_bitcast_fusion.refs_1_, bf16[192,192]{1,0:T(8,128)(2,1)} %refs_2_.1, bf16[512,768]{1,0:T(8,128)(2,1)} %refs_3_.1), custom_call_target="tpu_custom_call" | custom-call | tf_op jit(solution)/shard_map/gather_first/pallas_call | solution.py:382
  37.2 0.8 reshape.161
  38.3 1.8 convert_reduce_fusion
  40.1 0.6 fusion.9
  40.9 1.3 add_convert_fusion.3
  42.3 1.2 copy-done.1
  43.5 0.4 fusion.24
  44.0 1.4 copy.58
  45.5 1.6 fusion.61
  47.1 1.0 bitcast_reduce_fusion
  48.1 1.0 fusion.5
  49.2 1.6 copy-done
  50.8 1.9 fusion.83
  52.8 20.9 %gather_mixed.1 = (bf16[768,768]{1,0:T(8,128)(2,1)}, bf16[768,768]{1,0:T(8,128)(2,1)}, bf16[768,512]{1,0:T(8,128)(2,1)}) custom-call(bf16[192,768]{1,0:T(8,128)(2,1)} %refs_0_.1, bf16[192,768]{1,0:T(8,128)(2,1)} %bitcast.134, bf16[192,512]{1,0:T(8,128)(2,1)} %bitcast.125), custom_call_target="tpu_custom_call" | custom-call | tf_op jit(solution)/shard_map/gather_mixed/pallas_call | solution.py:382
  73.7 2.0 fusion.84
  75.8 0.3 multiply_reduce_fusion.1
  76.5 6.5 %multiply_convert_fusion = (bf16[512,768]{1,0:T(8,128)(2,1)}, f32[512,768]{1,0:T(8,128)S(1)}, f32[512,768]{1,0:T(8,128)S(1)}) fusion(f32[768]{0:T(1024)S(1)} %convert_element_type.162, bf16[768,768]{1,0:T(8,128)(2,1)} %get-tuple-element.42, f32[512,768]{1,0:T(8,128)S(1)} %get-tuple-element.149, f32[768]{0:T(1024)S(1)} %add.189, f32[768]{0:T(1024)S(1)} %mul.204, ...), kind=kOutput, calls=%fused_computation.61 | convolution fusion | flops 631898112 | bytes 6697984 | tf_op jit(solution)/shard_map/dot_general | solution.py:29
  82.9 1.2 convert_reduce_fusion.4
  84.2 1.7 convolution_convert_fusion.4.refs_2_
  85.9 2.1 convolution_convert_fusion.1.refs_0_
  88.0 3.3 %fusion.50.refs_1_ = bf16[768,768]{1,0:T(8,128)(2,1)} fusion(bf16[512,768]{1,0:T(8,128)(2,1)} %get-tuple-element.46, bf16[512,768]{1,0:T(8,128)(2,1)} %param.18), kind=kOutput, calls=%fused_computation.88 | convolution fusion | flops 604569600 | bytes 2752512 | tf_op jit(solution)/shard_map/dot_general | solution.py:33
  91.2 40.1 %grad_second.1 = (bf16[192,768]{1,0:T(8,128)(2,1)}, bf16[192,768]{1,0:T(8,128)(2,1)}, bf16[512,768]{1,0:T(8,128)(2,1)}) custom-call(bf16[768,768]{1,0:T(8,128)(2,1)} %convolution_convert_fusion.1.refs_0_, bf16[768,768]{1,0:T(8,128)(2,1)} %fusion.50.refs_1_, bf16[512,768]{1,0:T(8,128)(2,1)} %convolution_convert_fusion.4.refs_2_), custom_call_target="tpu_custom_call" | custom-call | tf_op jit(solution)/shard_map/grad_second/pallas_call | solution.py:382
  131.3 0.8 convolution_convert_fusion.3
  132.2 0.8 constant_dynamic-slice_fusion.3
  133.0 3.8 %collective-permute-start = (bf16[128,768]{1,0:T(8,128)(2,1)}, bf16[128,768]{1,0:T(8,128)(2,1)}, u32[]{:S(2)}, u32[]{:S(2)}) collective-permute-start(bf16[128,768]{1,0:T(8,128)(2,1)} %get-tuple-element.125), channel_id=1, source_target_pairs={{0,1},{1,2},{2,3},{3,0},{4,5},{5,6},{6,7},{7,4},{8,9},{9,10},{10,1... | collective-permute-start | bytes 589832 | tf_op jit(solution)/shard_map/ppermute | solution.py:536
  136.8 2.3 collective-permute-start.1
  139.2 1.5 fusion.22
  140.7 0.8 fusion.30
  141.5 3.7 %convert_reduce_fusion.5 = (f32[768]{0:T(1024)S(1)}, f32[512,768]{1,0:T(8,128)}, f32[768]{0:T(1024)S(1)}) fusion(f32[512]{0:T(512)S(1)} %get-tuple-element.153, f32[512,768]{1,0:T(8,128)} %copy-done.2, f32[512]{0:T(512)S(1)} %broadcast_multiply_fusion.5, f32[512]{0:T(512)S(1)} %get-tuple-element.154, f32[768]{0:T(1024)S(1)} %mul.204, ...), kind=kLoop, calls=%fused_computation.59 | loop fusion | flops 5503488 | bytes 4736000 | tf_op jit(solution)/shard_map/reduce_sum | solution.py:581
  145.3 2.2 convolution_convert_fusion.7
  147.6 4.7 %fusion.54 = bf16[3,64,1024]{2,1,0:T(8,128)(2,1)} fusion(bf16[512,3,64]{0,2,1:T(8,128)(2,1)S(1)} %bitcast.121, f32[3,1024,512]{2,1,0:T(8,128)} %copy-done, f32[512,3]{0,1:T(4,128)S(1)} %log_add_fusion), kind=kOutput, calls=%fused_computation.95 | convolution fusion | flops 206241792 | bytes 6887424 | tf_op jit(solution)/shard_map/qhk,qhd->khd/dot_general | solution.py:550
  152.3 1.8 fusion.1
  154.1 1.1 fusion.53
  155.2 1.3 fusion.60
  156.6 1.0 convolution_convert_fusion.6
  157.9 1.2 copy.63
  159.1 1.8 copy.65
  160.8 1.9 copy.67
  162.8 1.2 pad_maximum_fusion.1.refs_0_
  164.0 2.3 add_convert_fusion.4
  166.3 18.2 %grad_kv.1 = (bf16[512,384]{1,0:T(8,128)(2,1)}, bf16[512,768]{1,0:T(8,128)(2,1)}) custom-call(bf16[1024,384]{1,0:T(8,128)(2,1)} %pad_maximum_fusion.1.refs_0_, bf16[128,768]{1,0:T(8,128)(2,1)} %get-tuple-element.155.refs_1_), custom_call_target="tpu_custom_call" | custom-call | tf_op jit(solution)/shard_map/grad_kv/pallas_call | solution.py:382
  184.5 1.3 convert_reduce_fusion.6
  185.8 2.8 %convolution_convert_fusion.5.refs_1_ = bf16[512,768]{1,0:T(8,128)(2,1)} fusion(bf16[768,576]{1,0:T(8,128)(2,1)S(1)} %copy-done.29, bf16[512,384]{1,0:T(8,128)(2,1)} %get-tuple-element.48, bf16[512,192]{1,0:T(8,128)(2,1)S(1)} %copy-done.16), kind=kOutput, calls=%fused_computation.91 | convolution fusion | flops 454557696 | bytes 2260992 | tf_op jit(solution)/shard_map/dot_general | solution.py:39
  188.6 2.0 convolution_convert_fusion.2
  190.7 0.6 reshape.170.refs_5_
  191.3 1.5 copy.66
  192.8 2.2 pad_maximum_fusion.refs_0_
  195.1 44.6 %grad_first.1 = (f32[192,768]{1,0:T(8,128)}, bf16[512,768]{1,0:T(8,128)(2,1)}, f32[8,768]{1,0:T(8,128)}, f32[192,768]{1,0:T(8,128)}, f32[192,768]{1,0:T(8,128)}, /*index=5*/f32[8,640]{1,0:T(8,128)}) custom-call(bf16[768,768]{1,0:T(8,128)(2,1)} %pad_maximum_fusion.refs_0_, bf16[512,768]{1,0:T(8,128)(2,1)} %convolution_convert_fusion.5.refs_1_, ...), custom_call_target="tpu_custom_call" | custom-call | tf_op jit(solution)/shard_map/grad_first/pallas_call | solution.py:382
  239.7 0.7 reshape.171
  240.4 0.6 slice.135
  241.0 0.6 fusion.80
  241.6 0.8 slice.104
  242.5 0.6 fusion.81
  243.1 1.8 fusion.40
  245.0 0.9 slice_bitcast_fusion
  245.9 0.8 copy.68
  246.7 1.7 multiply_add_fusion
  248.6 1.1 add_convert_fusion
  249.7 0.8 copy.76
  250.5 0.8 copy.77
  (102 shorter events, 2.1 us)
Async XLA Ops:
  37.2 2.9 %copy-start.6 = (bf16[1024,768]{1,0:T(8,128)(2,1)S(1)}, bf16[1024,768]{1,0:T(8,128)(2,1)}, u32[]{:S(2)}) copy-start(bf16[1024,768]{1,0:T(8,128)(2,1)} %get-tuple-element.37) | copy-start | bytes 4718596
  38.3 2.5 copy-start.24
  38.3 2.6 %copy-start.28 = (bf16[768,576]{1,0:T(8,128)(2,1)S(1)}, bf16[768,576]{1,0:T(8,128)(2,1)}, u32[]{:S(2)}) copy-start(bf16[768,576]{1,0:T(8,128)(2,1)} %get-tuple-element.39) | copy-start | bytes 2654212
  42.2 1.3 copy-start.1
  42.2 1.6 copy-start.30
  42.2 1.8 copy-start.14
  42.3 4.8 %copy-start.7 = (bf16[1024,192]{0,1:T(8,128)(2,1)}, bf16[1024,192]{0,1:T(8,128)(2,1)S(1)}, u32[]{:S(2)}) copy-start(bf16[1024,192]{0,1:T(8,128)(2,1)S(1)} %get-tuple-element.128) | copy-start | bytes 1179652
  48.1 2.7 %copy-start = (f32[3,1024,512]{2,1,0:T(8,128)}, f32[3,1024,512]{2,1,0:T(8,128)S(1)}, u32[]{:S(2)}) copy-start(f32[3,1024,512]{2,1,0:T(8,128)S(1)} %get-tuple-element.145) | copy-start | bytes 18874372
  50.8 22.9 %copy-start.11 = (bf16[4,768,192]{1,2,0:T(8,128)(2,1)S(1)}, bf16[4,768,192]{1,2,0:T(8,128)(2,1)}, u32[]{:S(2)}) copy-start(bf16[4,768,192]{1,2,0:T(8,128)(2,1)} %copy.58) | copy-start | bytes 3538948
  75.8 10.1 %copy-start.2 = (f32[512,768]{1,0:T(8,128)}, f32[512,768]{1,0:T(8,128)S(1)}, u32[]{:S(2)}) copy-start(f32[512,768]{1,0:T(8,128)S(1)} %get-tuple-element.149) | copy-start | bytes 4718596
  75.8 0.7 copy-start.23
  76.5 6.5 %copy-start.19 = (bf16[512,768]{1,0:T(8,128)(2,1)S(1)}, bf16[512,768]{1,0:T(8,128)(2,1)}, u32[]{:S(2)}) copy-start(bf16[512,768]{1,0:T(8,128)(2,1)} %param.18) | copy-start | bytes 2359300
  76.5 6.5 %copy-start.25 = (bf16[768,768]{1,0:T(8,128)(2,1)S(1)}, bf16[768,768]{1,0:T(8,128)(2,1)}, u32[]{:S(2)}) copy-start(bf16[768,768]{1,0:T(8,128)(2,1)} %get-tuple-element.43) | copy-start | bytes 3538948
  82.9 1.3 copy-start.27
  91.2 40.1 %copy-start.26 = (bf16[768,768]{1,0:T(8,128)(2,1)S(1)}, bf16[768,768]{1,0:T(8,128)(2,1)}, u32[]{:S(2)}) copy-start(bf16[768,768]{1,0:T(8,128)(2,1)} %get-tuple-element.43) | copy-start | bytes 3538948
  91.2 40.1 %copy-start.31 = (bf16[512,768]{1,0:T(8,128)(2,1)S(1)}, bf16[512,768]{1,0:T(8,128)(2,1)}, u32[]{:S(2)}) copy-start(bf16[512,768]{1,0:T(8,128)(2,1)} %get-tuple-element.46) | copy-start | bytes 2359300
  132.2 8.5 %copy-start.17 = (bf16[512,768]{1,0:T(8,128)(2,1)}, bf16[512,768]{1,0:T(8,128)(2,1)S(1)}, u32[]{:S(2)}) copy-start(bf16[512,768]{1,0:T(8,128)(2,1)S(1)} %convolution_convert_fusion.3) | copy-start | bytes 2359300
  132.2 8.5 %copy-start.3 = (f32[512,768]{1,0:T(8,128)S(1)}, f32[512,768]{1,0:T(8,128)}, u32[]{:S(2)}) copy-start(f32[512,768]{1,0:T(8,128)} %copy-done.2) | copy-start | bytes 4718596
  132.2 8.5 %copy-start.10 = (bf16[512,768]{1,0:T(8,128)(2,1)S(1)}, bf16[512,768]{1,0:T(8,128)(2,1)}, u32[]{:S(2)}) copy-start(bf16[512,768]{1,0:T(8,128)(2,1)} %get-tuple-element.45) | copy-start | bytes 2359300
  133.0 30.9 %collective-permute-start = (bf16[128,768]{1,0:T(8,128)(2,1)}, bf16[128,768]{1,0:T(8,128)(2,1)}, u32[]{:S(2)}, u32[]{:S(2)}) collective-permute-start(bf16[128,768]{1,0:T(8,128)(2,1)} %get-tuple-element.125), channel_id=1, source_target_pairs={{0,1},{1,2},{2,3},{3,0},{4,5},{5,6},{6,7},{7,4},{8,9},{9,10},{10,1... | collective-permute-start | bytes 589832 | tf_op jit(solution)/shard_map/ppermute | solution.py:536
  136.8 27.1 %collective-permute-start.1 = (bf16[128,768]{1,0:T(8,128)(2,1)}, bf16[128,768]{1,0:T(8,128)(2,1)}, u32[]{:S(2)}, u32[]{:S(2)}) collective-permute-start(bf16[128,768]{1,0:T(8,128)(2,1)} %get-tuple-element.127), channel_id=1, source_target_pairs={{0,2},{1,3},{2,0},{3,1},{4,6},{5,7},{6,4},{7,5},{8,10},{9,11},{10,... | collective-permute-start | bytes 589832 | tf_op jit(solution)/shard_map/ppermute | solution.py:536
  139.1 24.9 %collective-permute-start.2 = (bf16[128,768]{1,0:T(8,128)(2,1)}, bf16[128,768]{1,0:T(8,128)(2,1)}, u32[]{:S(2)}, u32[]{:S(2)}) collective-permute-start(bf16[128,768]{1,0:T(8,128)(2,1)} %get-tuple-element.126), channel_id=1, source_target_pairs={{0,3},{1,0},{2,1},{3,2},{4,7},{5,4},{6,5},{7,6},{8,11},{9,8},{10,9... | collective-permute-start | bytes 589832 | tf_op jit(solution)/shard_map/ppermute | solution.py:536
  140.7 11.6 %slice-start = ((s8[6291456]{0:T(1024)(128)(4,1)}), s8[2097152]{0:T(1024)(128)(4,1)S(1)}, s32[]{:S(2)}) async-start(s8[6291456]{0:T(1024)(128)(4,1)} %bitcast.114), calls=%async_computation | async-start | bytes 4194304
  145.3 2.3 copy-start.13
  145.3 7.1 %slice-start.1 = ((s8[6291456]{0:T(1024)(128)(4,1)}), s8[4194304]{0:T(1024)(128)(4,1)S(1)}, s32[]{:S(2)}) async-start(s8[6291456]{0:T(1024)(128)(4,1)} %bitcast.114), calls=%async_computation.1 | async-start | bytes 8388608
  154.1 1.1 copy-start.8
  155.2 1.4 copy-start.5
  155.2 1.4 copy-start.12
  164.0 20.5 %copy-start.16 = (bf16[512,192]{1,0:T(8,128)(2,1)S(1)}, bf16[512,192]{1,0:T(8,128)(2,1)}, u32[]{:S(2)}) copy-start(bf16[512,192]{1,0:T(8,128)(2,1)} %copy.65) | copy-start | bytes 589828
  164.0 21.8 %copy-start.29 = (bf16[768,576]{1,0:T(8,128)(2,1)S(1)}, bf16[768,576]{1,0:T(8,128)(2,1)}, u32[]{:S(2)}) copy-start(bf16[768,576]{1,0:T(8,128)(2,1)} %get-tuple-element.39) | copy-start | bytes 2654212
  185.8 2.8 %copy-start.22 = (bf16[512,384]{1,0:T(8,128)(2,1)S(1)}, bf16[512,384]{1,0:T(8,128)(2,1)}, u32[]{:S(2)}) copy-start(bf16[512,384]{1,0:T(8,128)(2,1)} %get-tuple-element.48) | copy-start | bytes 1179652
  241.6 3.3 %copy-start.15 = (f32[192,768]{1,0:T(8,128)S(1)}, f32[192,768]{1,0:T(8,128)}, u32[]{:S(2)}) copy-start(f32[192,768]{1,0:T(8,128)} %get-tuple-element.54) | copy-start | bytes 1769476
  243.1 3.6 %copy-start.9 = (bf16[512,768]{1,0:T(8,128)(2,1)S(1)}, bf16[512,768]{1,0:T(8,128)(2,1)}, u32[]{:S(2)}) copy-start(bf16[512,768]{1,0:T(8,128)(2,1)} %get-tuple-element.51) | copy-start | bytes 2359300
  246.7 1.7 copy-start.4
  246.7 1.9 copy-start.18
  248.6 1.1 copy-start.21
  248.6 1.9 copy-start.20
